TPU v7x, 128 devices: a whole 4x4x4 slice. The times are simulated.
128 devices in a mesh: section: 4 (over z), dp: 4 (over x_hi, core), tensor: 8 (over x_lo, y).
Axes of the slice: x: 4 (x_hi: 2, x_lo: 2; x = x_hi * 2 + x_lo), y: 4, z: 4, core: 2. Of those that a mesh axis runs over, the one named last changes fastest.
Arguments:
- inputs: bfloat16 [8, 128, 8192], P(None, 'dp', ('section', 'tensor')), may hold values from -6 to 6
- gate_wide: bfloat16 [8192, 14336], P('section', 'tensor'), may hold values from -0.0625 to 0.0625
- up_wide: bfloat16 [8192, 14336], P('section', 'tensor'), may hold values from -0.0625 to 0.0625
- down_wide: bfloat16 [14336, 8192], P('tensor', 'section'), may hold values from -0.09375 to 0.09375
- width_wide: int32 [1], replicated, may hold values from 7168 to 14336
- gate_narrow: bfloat16 [8192, 7168], P(('section', 'tensor'), 'dp'), may hold values from -0.0625 to 0.0625
- up_narrow: bfloat16 [8192, 7168], P(('section', 'tensor'), 'dp'), may hold values from -0.0625 to 0.0625
- down_narrow: bfloat16 [7168, 8192], P('dp', ('section', 'tensor')), may hold values from -0.125 to 0.125
- width_narrow: int32 [1], replicated, may hold values from 3584 to 7168
- cotangent: bfloat16 [8, 128, 8192], P('tensor', 'dp', 'section'), may hold values from -6 to 6
Outputs:
- outputs: bfloat16 [8, 128, 8192], P('tensor', 'dp', 'section')
- input_grad: bfloat16 [8, 128, 8192], P(None, 'dp', ('section', 'tensor'))
All inputs are finite; a program needn't handle non-finite values.
Results may differ from a plain program's by a relative error of at most 0.017.
Values may be sent and summed in bfloat16 or wider, within the bound.
No kernel may reach another device: no remote copies, remote signals or barrier semaphores. Data moves between devices by JAX's collectives and lax.ppermute only.
A program may use at most 128 MiB of HBM per device.

v0:
```python
import jax
import jax.numpy as jnp
from jax import lax
from jax.sharding import PartitionSpec as P


def against(left, weight):
    return lax.dot_general(
        left, weight, (((1,), (1,)), ((), ())), preferred_element_type=jnp.float32
    )


def hidden_of(gate, upper, mask):
    sigma = jax.nn.sigmoid(gate)
    return (gate * sigma * upper * mask).astype(jnp.bfloat16)


def grads_of(dhid, gate, upper, mask):
    sigma = jax.nn.sigmoid(gate)
    dgate = (dhid * upper * sigma * (1.0 + gate * (1.0 - sigma)) * mask).astype(jnp.bfloat16)
    dup = (dhid * gate * sigma * mask).astype(jnp.bfloat16)
    return jnp.concatenate([dgate, dup], axis=1)


def both_terms(rows, gate_w, up_w):
    return jnp.concatenate(
        [
            jnp.dot(rows, gate_w, preferred_element_type=jnp.float32),
            jnp.dot(rows, up_w, preferred_element_type=jnp.float32),
        ],
        axis=1,
    )


def body(
    inputs,
    gate_wide,
    up_wide,
    down_wide,
    width_wide,
    gate_narrow,
    up_narrow,
    down_narrow,
    width_narrow,
    cotangent,
):
    wide_units = gate_wide.shape[1]
    narrow_units = gate_narrow.shape[1]
    blocks = inputs.shape[0]
    quarter = inputs.shape[1]
    mask_a = (
        lax.axis_index("tensor") * wide_units + jnp.arange(wide_units, dtype=jnp.int32)
        < width_wide[0]
    ).astype(jnp.float32)
    mask_b = (
        lax.axis_index("dp") * narrow_units + jnp.arange(narrow_units, dtype=jnp.int32)
        < width_narrow[0]
    ).astype(jnp.float32)
    rows_all = lax.all_gather(inputs, "tensor", axis=2, tiled=True)
    section_feats = rows_all.shape[2]
    flat_a = rows_all.reshape(blocks * quarter, section_feats)
    both_a = lax.psum_scatter(
        both_terms(flat_a, gate_wide, up_wide), "section", scatter_dimension=0, tiled=True
    )
    gate_a = both_a[:, :wide_units]
    upper_a = both_a[:, wide_units:]
    hidden_a = hidden_of(gate_a, upper_a, mask_a)
    partial_a = jnp.dot(
        lax.all_gather(hidden_a, "section", axis=0, tiled=True),
        down_wide,
        preferred_element_type=jnp.float32,
    )
    reduced_a = lax.psum_scatter(
        partial_a.reshape(blocks, quarter, section_feats), "tensor", scatter_dimension=2, tiled=True
    )
    middle = (inputs.astype(jnp.float32) + reduced_a).astype(jnp.bfloat16)
    moved = lax.all_to_all(middle, "tensor", split_axis=0, concat_axis=2, tiled=True)
    rows_b = lax.all_gather(moved, "dp", axis=1, tiled=True)
    tok_block = rows_b.shape[1]
    flat_b = rows_b.reshape(tok_block, section_feats)
    gate_full, up_full, down_full = (
        lax.all_gather(gate_narrow, "tensor", axis=0, tiled=True),
        lax.all_gather(up_narrow, "tensor", axis=0, tiled=True),
        lax.all_gather(down_narrow, "tensor", axis=1, tiled=True),
    )
    both_b = lax.psum_scatter(
        both_terms(flat_b, gate_full, up_full), "section", scatter_dimension=0, tiled=True
    )
    gate_b = both_b[:, :narrow_units]
    upper_b = both_b[:, narrow_units:]
    hidden_b = hidden_of(gate_b, upper_b, mask_b)
    partial_b = jnp.dot(
        lax.all_gather(hidden_b, "section", axis=0, tiled=True),
        down_full,
        preferred_element_type=jnp.float32,
    )
    reduced_b = lax.psum_scatter(
        partial_b.reshape(1, tok_block, section_feats), "dp", scatter_dimension=1, tiled=True
    )
    outputs = (moved.astype(jnp.float32) + reduced_b).astype(jnp.bfloat16)
    cot_rows = lax.all_gather(cotangent, "dp", axis=1, tiled=True).reshape(tok_block, section_feats)
    dhid_b = lax.psum_scatter(
        against(cot_rows, down_full), "section", scatter_dimension=0, tiled=True
    )
    pair_b = grads_of(dhid_b, gate_b, upper_b, mask_b)
    piece = lax.all_gather(pair_b, "section", axis=0, tiled=True)
    back_b = against(piece[:, :narrow_units], gate_full) + against(piece[:, narrow_units:], up_full)
    summed_b = lax.psum_scatter(
        back_b.reshape(1, tok_block, section_feats), "dp", scatter_dimension=1, tiled=True
    )
    middle_grad = (cotangent.astype(jnp.float32) + summed_b).astype(jnp.bfloat16)
    returned = lax.all_to_all(middle_grad, "tensor", split_axis=2, concat_axis=0, tiled=True)
    grad_rows = lax.all_gather(returned, "tensor", axis=2, tiled=True).reshape(
        blocks * quarter, section_feats
    )
    dhid_a = lax.psum_scatter(
        against(grad_rows, down_wide), "section", scatter_dimension=0, tiled=True
    )
    pair_a = grads_of(dhid_a, gate_a, upper_a, mask_a)
    piece = lax.all_gather(pair_a, "section", axis=0, tiled=True)
    back_a = against(piece[:, :wide_units], gate_wide) + against(piece[:, wide_units:], up_wide)
    summed_a = lax.psum_scatter(
        back_a.reshape(blocks, quarter, section_feats), "tensor", scatter_dimension=2, tiled=True
    )
    input_grad = (returned.astype(jnp.float32) + summed_a).astype(jnp.bfloat16)
    return (outputs, input_grad)


def solution(mesh):
    in_specs = (
        P(None, "dp", ("section", "tensor")),
        P("section", "tensor"),
        P("section", "tensor"),
        P("tensor", "section"),
        P(),
        P(("section", "tensor"), "dp"),
        P(("section", "tensor"), "dp"),
        P("dp", ("section", "tensor")),
        P(),
        P("tensor", "dp", "section"),
    )
    out_specs = (P("tensor", "dp", "section"), P(None, "dp", ("section", "tensor")))
    return jax.shard_map(body, mesh=mesh, in_specs=in_specs, out_specs=out_specs, check_vma=False)
```

profile of v0, /device:TPU:0, one launch (start us, length us, event | category | flops | bytes accessed | tf_op | source)
XLA Modules:
  0.0 740.6 jit_solution(12270934656157785988)
XLA Ops:
  7.9 41.4 %all-gather.8.cloned.1.call-done = bf16[8,32,2048]{2,1,0:T(8,128)(2,1)} async-done(((bf16[8,32,256]{2,1,0:T(8,128)(2,1)}), bf16[8,32,2048]{2,1,0:T(8,128)(2,1)}) %all-gather.8.cloned.1.call-update) | async-done | bytes 1048592 | tf_op jit(solution)/shard_map/all_gather | solution.py:59
  49.4 5.6 fusion.16
  55.1 2.1 fusion.17
  57.2 2.4 pad_maximum_fusion
  59.7 0.7 all-gather.14.cloned.1.call-update
  61.1 43.1 %reduce-scatter.9.cloned.1.call-done = f32[64,3584]{1,0:T(8,128)} async-done(((f32[256,3584]{1,0:T(8,128)}), f32[64,3584]{1,0:T(8,128)}) %reduce-scatter.9.cloned.1.call-update) | async-done | bytes 917520 | tf_op jit(solution)/shard_map/reduce_scatter | solution.py:62
  104.2 1.3 multiply_convert_fusion.2
  105.5 14.8 %all_gather.34 = bf16[256,1792]{1,0:T(8,128)(2,1)S(1)} all-gather(bf16[64,1792]{1,0:T(8,128)(2,1)S(1)} %multiply_convert_fusion.2), channel_id=1, replica_groups=mesh['section'=4,'dp'=4,'tensor'=8] {'section'}, dimensions={0}, use_global_device_ids=true | all-gather | bytes 1146880 | tf_op jit(solution)/shard_map/all_gather | solution.py:69
  120.3 6.6 fusion.18
  128.2 11.8 %all_gather.40 = bf16[1,128,2048]{2,1,0:T(8,128)(2,1)S(1)} all-gather(bf16[1,32,2048]{2,1,0:T(8,128)(2,1)S(1)} %copy-done.1), channel_id=1, replica_groups=mesh['section'=4,'dp'=4,'tensor'=8] {'dp'}, dimensions={1}, use_global_device_ids=true | all-gather | bytes 655360 | tf_op jit(solution)/shard_map/all_gather | solution.py:101
  140.0 56.3 %all-gather.14.cloned.1.call-done = bf16[1792,2048]{1,0:T(8,128)(2,1)} async-done(((bf16[1792,256]{1,0:T(8,128)(2,1)}), bf16[1792,2048]{1,0:T(8,128)(2,1)}) %all-gather.14.cloned.1.call-update) | async-done | bytes 7340048 | tf_op jit(solution)/shard_map/all_gather | solution.py:84
  196.3 6.6 fusion.4
  203.0 40.6 %reduce-scatter.11.cloned.1.call-done = f32[8,32,256]{2,1,0:T(8,128)} async-done(((f32[8,32,2048]{2,1,0:T(8,128)}), f32[8,32,256]{2,1,0:T(8,128)}) %reduce-scatter.11.cloned.1.call-update) | async-done | bytes 262160 | tf_op jit(solution)/shard_map/reduce_scatter | solution.py:73
  243.7 1.0 add_convert_fusion.2
  244.7 9.1 %all_to_all.36 = bf16[8,32,256]{2,1,0:T(8,128)(2,1)S(1)} all-to-all(bf16[8,32,256]{2,1,0:T(8,128)(2,1)S(1)} %add_convert_fusion.2), channel_id=1, replica_groups=mesh['section'=4,'dp'=4,'tensor'=8] {'tensor'}, dimensions={0} | all-to-all | bytes 262144 | tf_op jit(solution)/shard_map/all_to_all | solution.py:77
  253.8 11.8 %all_gather.35 = bf16[1,128,2048]{2,1,0:T(8,128)(2,1)S(1)} all-gather(bf16[1,32,2048]{2,1,0:T(8,128)(2,1)S(1)} %bitcast.68), channel_id=1, replica_groups=mesh['section'=4,'dp'=4,'tensor'=8] {'dp'}, dimensions={1}, use_global_device_ids=true | all-gather | bytes 655360 | tf_op jit(solution)/shard_map/all_gather | solution.py:78
  265.6 63.1 %all-gather.12.cloned.1.call-done = bf16[2048,1792]{1,0:T(8,128)(2,1)} async-done(((bf16[256,1792]{1,0:T(8,128)(2,1)}), bf16[2048,1792]{1,0:T(8,128)(2,1)}) %all-gather.12.cloned.1.call-update) | async-done | bytes 7340048 | tf_op jit(solution)/shard_map/all_gather | solution.py:83
  328.7 4.2 fusion.6
  332.9 77.9 %all-gather.10.cloned.1.call-done = bf16[2048,1792]{1,0:T(8,128)(2,1)} async-done(((bf16[256,1792]{1,0:T(8,128)(2,1)}), bf16[2048,1792]{1,0:T(8,128)(2,1)}) %all-gather.10.cloned.1.call-update) | async-done | bytes 7340048 | tf_op jit(solution)/shard_map/all_gather | solution.py:82
  410.8 4.2 fusion.8
  415.0 1.4 pad_maximum_fusion.1
  417.3 18.0 %reduce-scatter.17.cloned.1.call-done = f32[32,1792]{1,0:T(8,128)} async-done(((f32[128,1792]{1,0:T(8,128)}), f32[32,1792]{1,0:T(8,128)}) %reduce-scatter.17.cloned.1.call-update) | async-done | bytes 229392 | tf_op jit(solution)/shard_map/reduce_scatter | solution.py:102
  435.3 29.7 %reduce-scatter.13.cloned.1.call-done = f32[32,3584]{1,0:T(8,128)} async-done(((f32[128,3584]{1,0:T(8,128)}), f32[32,3584]{1,0:T(8,128)}) %reduce-scatter.13.cloned.1.call-update) | async-done | bytes 458768 | tf_op jit(solution)/shard_map/reduce_scatter | solution.py:86
  465.0 1.3 multiply_convert_fusion.4
  466.4 14.8 %all_gather.41 = bf16[128,3584]{1,0:T(8,128)(2,1)S(1)} all-gather(bf16[32,3584]{1,0:T(8,128)(2,1)S(1)} %pad_maximum_fusion.3), channel_id=1, replica_groups=mesh['section'=4,'dp'=4,'tensor'=8] {'section'}, dimensions={0}, use_global_device_ids=true | all-gather | bytes 1146880 | tf_op jit(solution)/shard_map/all_gather | solution.py:106
  481.2 5.7 fusion.11
  486.9 3.6 fusion
  490.6 31.5 %reduce-scatter.19.cloned.1.call-done = f32[1,32,2048]{2,1,0:T(8,128)} async-done(((f32[1,128,2048]{2,1,0:T(8,128)}), f32[1,32,2048]{2,1,0:T(8,128)}) %reduce-scatter.19.cloned.1.call-update) | async-done | bytes 262160 | tf_op jit(solution)/shard_map/reduce_scatter | solution.py:108
  522.1 1.0 add_convert_fusion
  523.0 0.7 copy.23
  524.3 11.5 %reduce = bf16[2048,32]{1,0:T(8,128)(2,1)S(1)} reduce(bf16[2048,1,32]{2,1,0:T(2,128)(2,1)S(1)} %bitcast.65, bf16[]{:T(256)} %broadcast.30), dimensions={1}, to_apply=%bitcast.39.reduce_sub_computation | reduce | bytes 262146
  536.3 10.7 %all_to_all.37 = bf16[8,2,4096]{2,1,0:T(2,128)(2,1)S(1)} all-to-all(bf16[8,2,4096]{2,1,0:T(2,128)(2,1)S(1)} %reshape.63), channel_id=1, replica_groups=mesh['section'=4,'dp'=4,'tensor'=8] {'tensor'}, dimensions={0} | all-to-all | bytes 262144 | tf_op jit(solution)/shard_map/all_to_all | solution.py:112
  549.0 35.9 %all-gather.18.cloned.1.call-done = bf16[8,1,32,2048]{3,0,2,1:T(8,128)(2,1)} async-done(((bf16[8,1,32,256]{3,0,2,1:T(8,128)(2,1)}), bf16[8,1,32,2048]{3,0,2,1:T(8,128)(2,1)}) %all-gather.18.cloned.1.call-update) | async-done | bytes 1048592 | tf_op jit(solution)/shard_map/all_gather | solution.py:113
  584.9 1.8 copy.25
  586.7 6.6 fusion.19
  593.4 29.5 %reduce-scatter.21.cloned.1.call-done = f32[64,1792]{1,0:T(8,128)} async-done(((f32[256,1792]{1,0:T(8,128)}), f32[64,1792]{1,0:T(8,128)}) %reduce-scatter.21.cloned.1.call-update) | async-done | bytes 458768 | tf_op jit(solution)/shard_map/reduce_scatter | solution.py:116
  622.9 1.3 multiply_convert_fusion.1
  624.1 0.8 pad_maximum_fusion.2
  625.0 13.5 %all_gather.38 = bf16[128,1792]{1,0:T(8,128)(2,1)S(1)} all-gather(bf16[32,1792]{1,0:T(8,128)(2,1)S(1)} %get-tuple-element.10), channel_id=1, replica_groups=mesh['section'=4,'dp'=4,'tensor'=8] {'section'}, dimensions={0}, use_global_device_ids=true | all-gather | bytes 573440 | tf_op jit(solution)/shard_map/all_gather | solution.py:93
  638.5 5.3 convolution_bitcast_fusion
  643.9 9.8 %all-gather.16.cloned.1.call-done = bf16[256,3584]{1,0:T(8,128)(2,1)} async-done(((bf16[64,3584]{1,0:T(8,128)(2,1)}), bf16[256,3584]{1,0:T(8,128)(2,1)}) %all-gather.16.cloned.1.call-update) | async-done | bytes 1835024 | tf_op jit(solution)/shard_map/all_gather | solution.py:120
  653.6 5.6 fusion.2
  659.2 5.2 convolution_add_fusion
  664.4 2.5 copy.26
  667.0 21.1 %reduce-scatter.15.cloned.1.call-done = f32[1,32,2048]{2,1,0:T(8,128)} async-done(((f32[1,128,2048]{2,1,0:T(8,128)}), f32[1,32,2048]{2,1,0:T(8,128)}) %reduce-scatter.15.cloned.1.call-update) | async-done | bytes 262160 | tf_op jit(solution)/shard_map/reduce_scatter | solution.py:97
  688.1 1.6 add_convert_fusion.1
  689.7 42.7 %reduce-scatter.23.cloned.1.call-done = f32[8,32,256]{2,0,1:T(8,128)} async-done(((f32[8,32,2048]{2,0,1:T(8,128)}), f32[8,32,256]{2,0,1:T(8,128)}) %reduce-scatter.23.cloned.1.call-update) | async-done | bytes 262160 | tf_op jit(solution)/shard_map/reduce_scatter | solution.py:122
  732.4 1.0 fusion.13
  (55 shorter events, 6.2 us)
Async XLA Ops:
  7.2 42.2 %all-gather.8.cloned.1.call-start = ((), (), s32[]{:S(2)}) async-start(), calls=%async_computation.10 | async-start | bytes 1179648 | tf_op jit(solution)/shard_map/all_gather | solution.py:59
  7.9 96.3 %reduce-scatter.9.cloned.1.call-start = ((), (), s32[]{:S(2)}) async-start(), calls=%async_computation.11 | async-start | bytes 4587520 | tf_op jit(solution)/shard_map/reduce_scatter | solution.py:62
  49.4 5.6 copy-start.3
  49.4 5.7 copy-start.5
  59.6 136.7 %all-gather.14.cloned.1.call-start = ((), (), s32[]{:S(2)}) async-start(), calls=%async_computation.16 | async-start | bytes 8257536 | tf_op jit(solution)/shard_map/all_gather | solution.py:84
  60.4 183.3 %reduce-scatter.11.cloned.1.call-start = ((), (), s32[]{:S(2)}) async-start(), calls=%async_computation.12 | async-start | bytes 2359296 | tf_op jit(solution)/shard_map/reduce_scatter | solution.py:73
  120.3 7.9 %copy-start.1 = (bf16[1,32,2048]{2,1,0:T(8,128)(2,1)S(1)}, bf16[1,32,2048]{2,1,0:T(8,128)(2,1)}, u32[]{:S(2)}) copy-start(bf16[1,32,2048]{2,1,0:T(8,128)(2,1)} %param.19) | copy-start | bytes 393220
  126.9 116.8 %copy-start.2 = (bf16[8,32,256]{2,1,0:T(8,128)(2,1)S(1)}, bf16[8,32,256]{2,1,0:T(8,128)(2,1)}, u32[]{:S(2)}) copy-start(bf16[8,32,256]{2,1,0:T(8,128)(2,1)} %param.10) | copy-start | bytes 393220
  126.9 201.7 %all-gather.12.cloned.1.call-start = ((), (), s32[]{:S(2)}) async-start(), calls=%async_computation.14 | async-start | bytes 8257536 | tf_op jit(solution)/shard_map/all_gather | solution.py:83
  127.5 283.3 %all-gather.10.cloned.1.call-start = ((), (), s32[]{:S(2)}) async-start(), calls=%async_computation.13 | async-start | bytes 8257536 | tf_op jit(solution)/shard_map/all_gather | solution.py:82
  128.1 307.2 %reduce-scatter.17.cloned.1.call-start = ((), (), s32[]{:S(2)}) async-start(), calls=%async_computation.18 | async-start | bytes 1146880 | tf_op jit(solution)/shard_map/reduce_scatter | solution.py:102
  203.0 262.0 %reduce-scatter.13.cloned.1.call-start = ((), (), s32[]{:S(2)}) async-start(), calls=%async_computation.15 | async-start | bytes 2293760 | tf_op jit(solution)/shard_map/reduce_scatter | solution.py:86
  416.4 70.5 %slice-start = ((s8[7340032]{0:T(1024)(128)(4,1)}), s8[3145728]{0:T(1024)(128)(4,1)S(1)}, s32[]{:S(2)}) async-start(s8[7340032]{0:T(1024)(128)(4,1)} %bitcast.62), calls=%async_computation.24 | async-start | bytes 6291456
  416.5 105.6 %reduce-scatter.19.cloned.1.call-start = ((), (), s32[]{:S(2)}) async-start(), calls=%async_computation.19 | async-start | bytes 1310720 | tf_op jit(solution)/shard_map/reduce_scatter | solution.py:108
  481.2 5.7 slice-start.1
  490.5 94.4 %all-gather.18.cloned.1.call-start = ((), (), s32[]{:S(2)}) async-start(), calls=%async_computation.23 | async-start | bytes 1179648 | tf_op jit(solution)/shard_map/all_gather | solution.py:113
  548.9 73.9 %reduce-scatter.21.cloned.1.call-start = ((), (), s32[]{:S(2)}) async-start(), calls=%async_computation.20 | async-start | bytes 2293760 | tf_op jit(solution)/shard_map/reduce_scatter | solution.py:116
  586.7 36.2 %copy-start = (f32[64,3584]{1,0:T(8,128)S(1)}, f32[64,3584]{1,0:T(8,128)}, u32[]{:S(2)}) copy-start(f32[64,3584]{1,0:T(8,128)} %reduce-scatter.9.cloned.1.call-done) | copy-start | bytes 2752516
  593.3 60.3 %all-gather.16.cloned.1.call-start = ((), (), s32[]{:S(2)}) async-start(), calls=%async_computation.21 | async-start | bytes 2293760 | tf_op jit(solution)/shard_map/all_gather | solution.py:120
  625.0 63.1 %reduce-scatter.15.cloned.1.call-start = ((), (), s32[]{:S(2)}) async-start(), calls=%async_computation.17 | async-start | bytes 1310720 | tf_op jit(solution)/shard_map/reduce_scatter | solution.py:97
  643.8 88.6 %reduce-scatter.23.cloned.1.call-start = ((), (), s32[]{:S(2)}) async-start(), calls=%async_computation.22 | async-start | bytes 2359296 | tf_op jit(solution)/shard_map/reduce_scatter | solution.py:122
  653.6 5.6 copy-start.4
Sparse Core Ops, SparseCore 0:
  9.6 39.7 all-gather.7
  59.8 44.3 reduce-scatter.8
  105.8 90.5 all-gather.13
  198.6 45.0 reduce-scatter.10
  245.2 83.4 all-gather.11
  330.2 80.5 all-gather.9
  413.2 22.0 reduce-scatter.16
  437.7 27.2 reduce-scatter.12
  490.6 31.3 reduce-scatter.18
  549.1 35.7 all-gather.17
  593.4 29.4 reduce-scatter.20
  625.1 28.4 all-gather.15
  656.5 31.5 reduce-scatter.14
  690.3 42.0 reduce-scatter.22
where the time goes:
time: 741 us
  waiting for transfers between devices  543 us (73%)
  blocking collectives  86.4 us (12%)
  matrix products  61.3 us (8%)
  other arithmetic  24.6 us (3%)
  between operations  15.6 us (2%)
  local copies, waits for them, and re-layouts  8.82 us (1%)
    all_gather x1, waiting for transfers between devices, body(): lax.all_gather(gate_narrow, 'tensor', axis=0, tiled=True)  77.9 us
    all_gather x1, waiting for transfers between devices, body(): lax.all_gather(up_narrow, 'tensor', axis=0, tiled=True)  63.1 us
    all_gather x1, waiting for transfers between devices, body(): lax.all_gather(down_narrow, 'tensor', axis=1, tiled=True)  56.3 us
    reduce_scatter x1, waiting for transfers between devices, body(): lax.psum_scatter(both_terms(flat_a, gate_wide, up_wide), 'section', scatt...  43.1 us
    reduce_scatter x1, waiting for transfers between devices, body(): lax.psum_scatter(back_a.reshape(blocks, quarter, section_feats), 'tensor'...  42.7 us
    all_gather x1, waiting for transfers between devices, body(): rows_all = lax.all_gather(inputs, 'tensor', axis=2, tiled=True)  41.4 us
    reduce_scatter x1, waiting for transfers between devices, body(): lax.psum_scatter(partial_a.reshape(blocks, quarter, section_feats), 'tens...  40.6 us
    all_gather x1, waiting for transfers between devices, body(): lax.all_gather(returned, 'tensor', axis=2, tiled=True)  35.9 us
  transfers between devices with their start and end apart: 14, of which 14 were waited for; matrix products, arithmetic and copies ran while one was open for 6% of the time, Pallas kernels for 0%

commit v1 on v0

v1 whole, which is shorter than its diff:
```python
import functools

import jax
import jax.numpy as jnp
from jax import lax
from jax.experimental import pallas as pl
from jax.experimental.pallas import tpu as pltpu
from jax.sharding import PartitionSpec as P

BF = jnp.bfloat16
F32 = jnp.float32
NT = (((1,), (1,)), ((), ()))


def ring(n, shift):
    return [(i, (i + shift) % n) for i in range(n)]


def send(parts, axis, n):
    return [lax.ppermute(p, axis, ring(n, r)) for r, p in zip(range(1, n), parts)]


def spread(own, axis, n):
    return [own] + send([own] * (n - 1), axis, n)


def whole(shape):
    zeros = (0,) * len(shape)
    return pl.BlockSpec(shape, lambda n, idx: zeros)


def fill_features(scratch, refs, t, slot):
    width = refs[0].shape[1]
    for k, ref in enumerate(refs):
        owner = lax.rem(t - k + 8, 8)
        at = pl.multiple_of(slot(owner, t) * width, width)
        scratch[:, pl.ds(at, width)] = ref[...]


def fill_rows(scratch, refs, me, n):
    rows = refs[0].shape[-2]
    for k, ref in enumerate(refs):
        at = pl.multiple_of(lax.rem(me - k + n, n) * rows, rows)
        if len(ref.shape) == 3:
            for g in range(ref.shape[0]):
                scratch[g, pl.ds(at, rows), :] = ref[g]
        else:
            scratch[pl.ds(at, rows), :] = ref[...]


def plain_slot(owner, t):
    return owner


def narrow_slot(owner, t):
    return ((owner ^ t) & 1) * 4 + owner // 2


def out_sections(value_ref, outs, s, place):
    rows = value_ref.shape[0] // 4
    for r, out in enumerate(outs):
        at = pl.multiple_of(lax.rem(s + r, 4) * rows, rows)
        place(out, value_ref[pl.ds(at, rows), :].astype(out.dtype))


def call(kernel, idx, operands, in_specs, out_shape, out_specs, grid, scratch, flops, moved):
    return pl.pallas_call(
        kernel,
        grid_spec=pltpu.PrefetchScalarGridSpec(
            num_scalar_prefetch=1,
            grid=(grid,),
            in_specs=in_specs,
            out_specs=out_specs,
            scratch_shapes=scratch,
        ),
        out_shape=out_shape,
        compiler_params=pltpu.CompilerParams(vmem_limit_bytes=32 << 20),
        cost_estimate=pl.CostEstimate(flops=flops, bytes_accessed=moved, transcendentals=0),
    )(idx, *operands)


def gate_up(idx, chunks, gate_w, up_w, narrow):
    tokens, width = chunks[0].shape
    feats = 8 * width
    units = gate_w.shape[-1]
    block = 128 if narrow else 256
    steps = units // block
    rows = tokens // 4
    mid_rows = tokens // 8

    def kernel(idx_ref, *refs):
        xs, g_ref, u_ref = refs[:8], refs[8], refs[9]
        outs = refs[10:14]
        mid, lhs, val = refs[14], refs[15], refs[16]
        s, t = idx_ref[0], idx_ref[1]

        @pl.when(pl.program_id(0) == 0)
        def _():
            fill_features(lhs, xs, t, narrow_slot if narrow else plain_slot)
            at = pl.multiple_of(t * mid_rows, mid_rows)
            for k, ref in enumerate(xs):
                owner = lax.rem(t - k + 8, 8)
                to = pl.multiple_of(owner * width, width)
                mid[:, pl.ds(to, width)] = ref[pl.ds(at, mid_rows), :]

        if narrow:
            gw = [g_ref[:, j].reshape(feats // 2, block) for j in range(2)]
            uw = [u_ref[:, j].reshape(feats // 2, block) for j in range(2)]
            w = jnp.concatenate(
                [jnp.concatenate(gw, axis=0), jnp.concatenate(uw, axis=0)], axis=1
            )
            val[...] = jnp.dot(lhs[...], w, preferred_element_type=F32)
        else:
            val[:, :block] = jnp.dot(lhs[...], g_ref[...], preferred_element_type=F32)
            val[:, block:] = jnp.dot(lhs[...], u_ref[...], preferred_element_type=F32)

        def place(out, v):
            out[0] = v[:, :block]
            out[1] = v[:, block:]

        out_sections(val, outs, s, place)

    if narrow:
        w_specs = [
            pl.BlockSpec((4, 2, width, block), lambda n, idx: (0, 0, 0, n)),
            pl.BlockSpec((4, 2, width, block), lambda n, idx: (0, 1, 0, n)),
        ]
    else:
        w_specs = [pl.BlockSpec((feats, block), lambda n, idx: (0, n))] * 2
    out_spec = pl.BlockSpec((2, rows, block), lambda n, idx: (0, 0, n))
    res = call(
        kernel,
        idx,
        (*chunks, gate_w, up_w),
        [whole(chunks[0].shape)] * 8 + w_specs,
        [jax.ShapeDtypeStruct((2, rows, units), F32)]
        + [jax.ShapeDtypeStruct((2, rows, units), BF)] * 3
        + [jax.ShapeDtypeStruct((mid_rows, feats), BF)],
        [out_spec] * 4 + [whole((mid_rows, feats))],
        steps,
        [pltpu.VMEM((tokens, feats), BF), pltpu.VMEM((tokens, 2 * block), F32)],
        4 * tokens * feats * units,
        4 * feats * units,
    )
    return res[0], res[1:4], res[4]


def down_wide_part(idx, chunks, down_w):
    rows, units = chunks[0].shape
    tokens = 4 * rows
    feats = down_w.shape[1]
    width = feats // 8

    def kernel(idx_ref, *refs):
        hs, w_ref, outs, lhs = refs[:4], refs[4], refs[5:13], refs[13]
        step = pl.program_id(0)

        @pl.when(step == 0)
        def _():
            fill_rows(lhs, hs, idx_ref[0], 4)

        value = jnp.dot(lhs[...], w_ref[...], preferred_element_type=F32)
        for k in range(8):
            out = outs[k]

            @pl.when(step == (k + 7) % 8)
            def _(out=out):
                out[...] = value.astype(out.dtype)

    res = call(
        kernel,
        idx,
        (*chunks, down_w),
        [whole(chunks[0].shape)] * 4
        + [pl.BlockSpec((units, width), lambda n, idx: (0, lax.rem(idx[1] + n + 1, 8)))],
        [jax.ShapeDtypeStruct((tokens, width), F32)]
        + [jax.ShapeDtypeStruct((tokens, width), BF)] * 7,
        [whole((tokens, width))] * 8,
        8,
        [pltpu.VMEM((tokens, units), BF)],
        2 * tokens * feats * units,
        2 * feats * units,
    )
    return res[0], res[1:]


def down_narrow_part(idx, chunks, down_w):
    rows, units = chunks[0].shape
    tokens = 4 * rows
    width = down_w.shape[-1]
    feats = 8 * width
    mid_rows = tokens // 8

    def kernel(idx_ref, *refs):
        hs, w_ref, outs, lhs, acc = refs[:4], refs[4], refs[5:13], refs[13], refs[14]
        step = pl.program_id(0)
        t = idx_ref[1]

        @pl.when(step == 0)
        def _():
            fill_rows(lhs, hs, idx_ref[0], 4)

        owner = 2 * (step // 2) + ((step & 1) ^ (t & 1))
        at = pl.multiple_of(owner * width, width)
        acc[:, pl.ds(at, width)] = jnp.dot(lhs[...], w_ref[0, 0], preferred_element_type=F32)

        @pl.when(step == 7)
        def _():
            for k, out in enumerate(outs):
                row = pl.multiple_of(lax.rem(t + k, 8) * mid_rows, mid_rows)
                out[...] = acc[pl.ds(row, mid_rows), :].astype(out.dtype)

    res = call(
        kernel,
        idx,
        (*chunks, down_w),
        [whole(chunks[0].shape)] * 4
        + [pl.BlockSpec((1, 1, units, width), lambda n, idx: (n // 2, n & 1, 0, 0))],
        [jax.ShapeDtypeStruct((mid_rows, feats), F32)]
        + [jax.ShapeDtypeStruct((mid_rows, feats), BF)] * 7,
        [whole((mid_rows, feats))] * 8,
        8,
        [pltpu.VMEM((tokens, units), BF), pltpu.VMEM((tokens, feats), F32)],
        2 * tokens * feats * units,
        2 * feats * units,
    )
    return res[0], res[1:]


def hidden_grad_wide(idx, chunks, down_w):
    tokens, width = chunks[0].shape
    feats = 8 * width
    units = down_w.shape[0]
    block = 256
    rows = tokens // 4

    def kernel(idx_ref, *refs):
        xs, w_ref, outs, lhs, val = refs[:8], refs[8], refs[9:13], refs[13], refs[14]
        s, t = idx_ref[0], idx_ref[1]

        @pl.when(pl.program_id(0) == 0)
        def _():
            fill_features(lhs, xs, t, plain_slot)

        val[...] = lax.dot_general(lhs[...], w_ref[...], NT, preferred_element_type=F32)

        def place(out, v):
            out[...] = v

        out_sections(val, outs, s, place)

    res = call(
        kernel,
        idx,
        (*chunks, down_w),
        [whole(chunks[0].shape)] * 8 + [pl.BlockSpec((block, feats), lambda n, idx: (n, 0))],
        [jax.ShapeDtypeStruct((rows, units), F32)]
        + [jax.ShapeDtypeStruct((rows, units), BF)] * 3,
        [pl.BlockSpec((rows, block), lambda n, idx: (0, n))] * 4,
        units // block,
        [pltpu.VMEM((tokens, feats), BF), pltpu.VMEM((tokens, block), F32)],
        2 * tokens * feats * units,
        2 * feats * units,
    )
    return res[0], res[1:]


def hidden_grad_narrow(idx, chunks, down_w):
    mid_rows, feats = chunks[0].shape
    tokens = 8 * mid_rows
    width = feats // 8
    units = down_w.shape[2]
    block = 128
    rows = tokens // 4

    def kernel(idx_ref, *refs):
        xs, w_ref, outs, own, lhs, val = (
            refs[:8], refs[8], refs[9:13], refs[13], refs[14], refs[15],
        )
        s, t = idx_ref[0], idx_ref[1]

        @pl.when(pl.program_id(0) == 0)
        def _():
            fill_rows(lhs, xs, t, 8)
            own[...] = lhs[:, pl.ds(pl.multiple_of(t * width, width), width)]

        total = None
        for f in range(4):
            for j in range(2):
                owner = 2 * f + (j ^ (t & 1))
                left = lhs[:, pl.ds(pl.multiple_of(owner * width, width), width)]
                term = lax.dot_general(left, w_ref[f, j], NT, preferred_element_type=F32)
                total = term if total is None else total + term
        val[...] = total

        def place(out, v):
            out[...] = v

        out_sections(val, outs, s, place)

    res = call(
        kernel,
        idx,
        (*chunks, down_w),
        [whole(chunks[0].shape)] * 8
        + [pl.BlockSpec((4, 2, block, width), lambda n, idx: (0, 0, n, 0))],
        [jax.ShapeDtypeStruct((rows, units), F32)]
        + [jax.ShapeDtypeStruct((rows, units), BF)] * 3
        + [jax.ShapeDtypeStruct((tokens, width), BF)],
        [pl.BlockSpec((rows, block), lambda n, idx: (0, n))] * 4 + [whole((tokens, width))],
        units // block,
        [pltpu.VMEM((tokens, feats), BF), pltpu.VMEM((tokens, block), F32)],
        2 * tokens * feats * units,
        2 * feats * units,
    )
    return res[0], res[1:4], res[4]


def input_back(idx, chunks, gate_w, up_w, narrow):
    _, rows, units = chunks[0].shape
    tokens = 4 * rows
    width = 256
    feats = 8 * width

    def kernel(idx_ref, *refs):
        ps, g_ref, u_ref, outs, lhs = refs[:4], refs[4], refs[5], refs[6:14], refs[14]
        step = pl.program_id(0)

        @pl.when(step == 0)
        def _():
            fill_rows(lhs, ps, idx_ref[0], 4)

        gw = g_ref[0, 0] if narrow else g_ref[...]
        uw = u_ref[0, 0] if narrow else u_ref[...]
        value = lax.dot_general(lhs[0], gw, NT, preferred_element_type=F32)
        value += lax.dot_general(lhs[1], uw, NT, preferred_element_type=F32)
        for k in range(8):
            out = outs[k]

            @pl.when(step == (k + 7) % 8)
            def _(out=out):
                out[...] = value.astype(out.dtype)

    def dest(n, idx):
        return lax.rem(idx[1] + n + 1, 8)

    if narrow:
        w_specs = [
            pl.BlockSpec(
                (1, 1, width, units),
                lambda n, idx: (dest(n, idx) // 2, (dest(n, idx) ^ idx[1]) & 1, 0, 0),
            ),
            pl.BlockSpec(
                (1, 1, width, units),
                lambda n, idx: (dest(n, idx) // 2, 2 + ((dest(n, idx) ^ idx[1]) & 1), 0, 0),
            ),
        ]
    else:
        w_specs = [pl.BlockSpec((width, units), lambda n, idx: (dest(n, idx), 0))] * 2
    res = call(
        kernel,
        idx,
        (*chunks, gate_w, up_w),
        [whole(chunks[0].shape)] * 4 + w_specs,
        [jax.ShapeDtypeStruct((tokens, width), F32)]
        + [jax.ShapeDtypeStruct((tokens, width), BF)] * 7,
        [whole((tokens, width))] * 8,
        8,
        [pltpu.VMEM((2, tokens, units), BF)],
        4 * tokens * feats * units,
        4 * feats * units,
    )
    return res[0], res[1:]


def add_up(own, received):
    total = own
    for r in received:
        total = total + r.astype(F32)
    return total


def hidden_of(gate, upper, mask):
    sigma = jax.nn.sigmoid(gate)
    return (gate * sigma * upper * mask).astype(BF)


def grads_of(dhid, gate, upper, mask):
    sigma = jax.nn.sigmoid(gate)
    dgate = (dhid * upper * sigma * (1.0 + gate * (1.0 - sigma)) * mask).astype(BF)
    dup = (dhid * gate * sigma * mask).astype(BF)
    return jnp.stack([dgate, dup])


def halves(w, axis, tensor):
    size = w.shape[axis] // 2
    parts = []
    for j in range(2):
        half = (tensor & 1) ^ j
        piece = lax.dynamic_slice_in_dim(w, half * size, size, axis)
        perm = [
            (d * 8 + t, (t // 2) * 8 + 2 * d + ((t & 1) ^ j)) for d in range(4) for t in range(8)
        ]
        parts.append(lax.ppermute(piece, ("dp", "tensor"), perm))
    return parts


def body(
    inputs,
    gate_wide,
    up_wide,
    down_wide,
    width_wide,
    gate_narrow,
    up_narrow,
    down_narrow,
    width_narrow,
    cotangent,
):
    section = lax.axis_index("section").astype(jnp.int32)
    tensor = lax.axis_index("tensor").astype(jnp.int32)
    idx = jnp.stack([section, tensor])
    units_a = gate_wide.shape[1]
    units_b = gate_narrow.shape[1] // 2
    mask_a = (
        tensor * units_a + jnp.arange(units_a, dtype=jnp.int32) < width_wide[0]
    ).astype(F32)
    mask_b = (
        tensor * units_b + jnp.arange(units_b, dtype=jnp.int32) < width_narrow[0]
    ).astype(F32)
    blocks, quarter, width = inputs.shape
    tokens = blocks * quarter
    own_in = inputs.reshape(tokens, width)

    x_chunks = spread(own_in, "tensor", 8)
    gu_b = jnp.stack(halves(gate_narrow, 1, tensor) + halves(up_narrow, 1, tensor))
    gu_b = lax.all_gather(gu_b, "dp", axis=0, tiled=False)
    down_b = jnp.stack(halves(down_narrow, 0, tensor))
    down_b = lax.all_gather(down_b, "dp", axis=0, tiled=False)

    own, parts, _ = gate_up(idx, x_chunks, gate_wide, up_wide, False)
    both_a = add_up(own, send(parts, "section", 4))
    hidden_a = hidden_of(both_a[0], both_a[1], mask_a)
    own, parts = down_wide_part(idx, spread(hidden_a, "section", 4), down_wide)
    middle = (own_in.astype(F32) + add_up(own, send(parts, "tensor", 8))).astype(BF)

    own, parts, mid_rows = gate_up(idx, spread(middle, "tensor", 8), gu_b, gu_b, True)
    both_b = add_up(own, send(parts, "section", 4))

    cot_chunks = spread(cotangent[0], "tensor", 8)
    own, parts, cot_own = hidden_grad_narrow(idx, cot_chunks, down_b)
    dhid_b = add_up(own, send(parts, "section", 4))

    pair_b = grads_of(dhid_b, both_b[0], both_b[1], mask_b)
    own, parts = input_back(idx, spread(pair_b, "section", 4), gu_b, gu_b, True)
    middle_grad = (cot_own.astype(F32) + add_up(own, send(parts, "tensor", 8))).astype(BF)

    hidden_b = hidden_of(both_b[0], both_b[1], mask_b)
    own, parts = down_narrow_part(idx, spread(hidden_b, "section", 4), down_b)
    outputs = (mid_rows.astype(F32) + add_up(own, send(parts, "tensor", 8))).astype(BF)

    own, parts = hidden_grad_wide(idx, spread(middle_grad, "tensor", 8), down_wide)
    dhid_a = add_up(own, send(parts, "section", 4))
    pair_a = grads_of(dhid_a, both_a[0], both_a[1], mask_a)
    own, parts = input_back(idx, spread(pair_a, "section", 4), gate_wide, up_wide, False)
    input_grad = (middle_grad.astype(F32) + add_up(own, send(parts, "tensor", 8))).astype(BF)
    return (
        outputs.reshape(1, quarter, outputs.shape[1]),
        input_grad.reshape(blocks, quarter, width),
    )


def solution(mesh):
    in_specs = (
        P(None, "dp", ("section", "tensor")),
        P("section", "tensor"),
        P("section", "tensor"),
        P("tensor", "section"),
        P(),
        P(("section", "tensor"), "dp"),
        P(("section", "tensor"), "dp"),
        P("dp", ("section", "tensor")),
        P(),
        P("tensor", "dp", "section"),
    )
    out_specs = (P("tensor", "dp", "section"), P(None, "dp", ("section", "tensor")))
    return jax.shard_map(body, mesh=mesh, in_specs=in_specs, out_specs=out_specs, check_vma=False)
```

time: 741 us -> 443 us (0.60)
  waiting for transfers between devices: 543 us -> 130 us
  starting transfers between devices: 0.57 us -> 226 us
  blocking collectives: 86.4 us -> 0 us
  matrix products: 61.3 us -> 0 us
  Pallas kernels: 0 us -> 43.1 us
  other arithmetic: 24.6 us -> 6.73 us
  local copies, waits for them, and re-layouts: 8.82 us -> 17.1 us
    all_gather x6 -> x2, waiting for transfers between devices: 284 us -> 0.01 us  [the longest x1 0.01 us: body(): gu_b = lax.all_gather(gu_b, 'dp', axis=0, tiled=False)]
    reduce_scatter x8 -> x0, waiting for transfers between devices: 256 us -> none  [the longest x1 43.1 us: body(): lax.psum_scatter(both_terms(flat_a, gate_wide, up_wide), 'section', scatt...]
    ppermute x0 -> x86, starting transfers between devices: none -> 226 us  [the longest x80 219 us: send(): lax.ppermute(p, axis, ring(n, r))]
    ppermute x0 -> x86, waiting for transfers between devices: none -> 130 us  [the longest x80 108 us: send(): lax.ppermute(p, axis, ring(n, r))]
    all_gather x5 -> x0, blocking collectives: 66.7 us -> none  [the longest x1 14.8 us: body(): piece = lax.all_gather(pair_b, 'section', axis=0, tiled=True)]
    dot_general x12 -> x0, matrix products: 61.3 us -> none  [the longest x6 33.3 us: against(): lax.dot_general(left, weight, (((1,), (1,)), ((), ())), preferred_element...]
    pallas_call x0 -> x8, Pallas kernels: none -> 43.1 us  [call(): pl.pallas_call(kernel, grid_spec=pltpu.PrefetchScalarGridSpec(num_scalar_...]
    all_to_all x2 -> x0, blocking collectives: 19.8 us -> none  [the longest x1 10.7 us: body(): lax.all_to_all(middle_grad, 'tensor', split_axis=2, concat_axis=0, tiled=...]
  transfers between devices with their start and end apart: 14 -> 88, of which waited for: 14 -> 38; matrix products, arithmetic and copies ran while one was open for 6% -> 1% of each run, Pallas kernels for 0% -> 8%
where the time goes in v1:
time: 443 us; the launch traced here: 439 us
  starting transfers between devices  226 us (51%)
  waiting for transfers between devices  130 us (29%)
  Pallas kernels  43.1 us (10%)
  local copies, waits for them, and re-layouts  17.1 us (4%)
  between operations  16 us (4%)
  other arithmetic  6.73 us (2%)
    ppermute x80, starting transfers between devices, send(): lax.ppermute(p, axis, ring(n, r))  219 us
    ppermute x80, waiting for transfers between devices, send(): lax.ppermute(p, axis, ring(n, r))  108 us
    pallas_call x8, Pallas kernels, call(): pl.pallas_call(kernel, grid_spec=pltpu.PrefetchScalarGridSpec(num_scalar_...  43.1 us
    ppermute x6, waiting for transfers between devices, halves(): parts.append(lax.ppermute(piece, ('dp', 'tensor'), perm))  22.1 us
    unnamed x38, local copies, waits for them, and re-layouts  15.6 us
  transfers between devices with their start and end apart: 88, of which 38 were waited for; matrix products, arithmetic and copies ran while one was open for 1% of the time, Pallas kernels for 8%

profile of v1, /device:TPU:0, one launch (start us, length us, event | category | flops | bytes accessed | tf_op | source)
XLA Modules:
  0.0 438.5 jit_solution(9323242074391342078)
XLA Ops:
  12.2 6.5 %collective-permute-done.30 = bf16[256,896]{1,0:T(8,128)(2,1)S(1)} collective-permute-done((bf16[256,896]{1,0:T(8,128)(2,1)S(1)}, bf16[256,896]{1,0:T(8,128)(2,1)S(1)}, u32[]{:S(2)}, u32[]{:S(2)}) %collective-permute-start.30) | collective-permute-done | bytes 458784 | tf_op jit(solution)/shard_map/ppermute | solution.py:404
  18.7 9.8 %collective-permute-done.28 = bf16[256,896]{1,0:T(8,128)(2,1)S(1)} collective-permute-done((bf16[256,896]{1,0:T(8,128)(2,1)S(1)}, bf16[256,896]{1,0:T(8,128)(2,1)S(1)}, u32[]{:S(2)}, u32[]{:S(2)}) %collective-permute-start.28) | collective-permute-done | bytes 458784 | tf_op jit(solution)/shard_map/ppermute | solution.py:404
  34.0 5.8 %collective-permute-done.38 = bf16[896,256]{1,0:T(8,128)(2,1)S(1)} collective-permute-done((bf16[896,256]{1,0:T(8,128)(2,1)S(1)}, bf16[896,256]{1,0:T(8,128)(2,1)S(1)}, u32[]{:S(2)}, u32[]{:S(2)}) %collective-permute-start.38) | collective-permute-done | bytes 458784 | tf_op jit(solution)/shard_map/ppermute | solution.py:404
  42.9 12.1 %collective-permute-start.1 = (bf16[256,256]{1,0:T(8,128)(2,1)S(1)}, bf16[256,256]{1,0:T(8,128)(2,1)S(1)}, u32[]{:S(2)}, u32[]{:S(2)}) collective-permute-start(bf16[256,256]{1,0:T(8,128)(2,1)S(1)} %bitcast.81), channel_id=1, source_target_pairs={{0,2},{1,3},{2,4},{3,5},{4,6},{5,7},{6,0},{7,1},{8,10},{9,11},{10,... | collective-permute-start | bytes 393224 | tf_op jit(solution)/shard_map/ppermute | solution.py:20
  55.0 70.0 %collective-permute-start.2 = (bf16[256,256]{1,0:T(8,128)(2,1)S(1)}, bf16[256,256]{1,0:T(8,128)(2,1)S(1)}, u32[]{:S(2)}, u32[]{:S(2)}) collective-permute-start(bf16[256,256]{1,0:T(8,128)(2,1)S(1)} %bitcast.82), channel_id=1, source_target_pairs={{0,3},{1,4},{2,5},{3,6},{4,7},{5,0},{6,1},{7,2},{8,11},{9,12},{10,... | collective-permute-start | bytes 393224 | tf_op jit(solution)/shard_map/ppermute | solution.py:20
  131.6 5.4 %collective-permute-done.5.refs_6_ = bf16[256,256]{1,0:T(8,128)(2,1)S(1)} collective-permute-done((bf16[256,256]{1,0:T(8,128)(2,1)S(1)}, bf16[256,256]{1,0:T(8,128)(2,1)S(1)}, u32[]{:S(2)}, u32[]{:S(2)}) %collective-permute-start.5) | collective-permute-done | bytes 131104 | tf_op jit(solution)/shard_map/ppermute | solution.py:20
  137.0 3.2 collective-permute-done.6.refs_7_
  140.2 3.1 copy-done.2
  143.3 3.1 copy-done.3
  146.4 8.1 %shard_map.113 = (f32[2,64,1792]{2,1,0:T(8,128)S(1)}, bf16[2,64,1792]{2,1,0:T(8,128)(2,1)S(1)}, bf16[2,64,1792]{2,1,0:T(8,128)(2,1)S(1)}, bf16[2,64,1792]{2,1,0:T(8,128)(2,1)S(1)}, bf16[32,2048]{1,0:T(8,128)(2,1)}) custom-call(s32[2]{0:T(128)S(1)} %pad_add_fusion.idx_ref, bf16[256,256]{1,0:T(8,128)(2,1)S(1)} %bitcast.87, ...), custom_call_target="tpu_custom_call" | custom-call | flops 3758096384 | bytes 14680064 | tf_op jit(solution)/shard_map/pallas_call | solution.py:67
  154.5 5.0 %collective-permute-start.9 = (bf16[2,64,1792]{2,1,0:T(8,128)(2,1)S(1)}, bf16[2,64,1792]{2,1,0:T(8,128)(2,1)S(1)}, u32[]{:S(2)}, u32[]{:S(2)}) collective-permute-start(bf16[2,64,1792]{2,1,0:T(8,128)(2,1)S(1)} %get-tuple-element.55), channel_id=1, source_target_pairs={{0,96},{32,0},{64,32},{96,64},{1,97},{33,1},{65,33},{97,65},{2,98}... | collective-permute-start | bytes 1376264 | tf_op jit(solution)/shard_map/ppermute | solution.py:20
  161.0 11.1 %collective-permute-done.9 = bf16[2,64,1792]{2,1,0:T(8,128)(2,1)S(1)} collective-permute-done((bf16[2,64,1792]{2,1,0:T(8,128)(2,1)S(1)}, bf16[2,64,1792]{2,1,0:T(8,128)(2,1)S(1)}, u32[]{:S(2)}, u32[]{:S(2)}) %collective-permute-start.9) | collective-permute-done | bytes 458784 | tf_op jit(solution)/shard_map/ppermute | solution.py:20
  172.1 3.5 collective-permute-done.7
  177.2 3.1 collective-permute-start.11
  180.5 7.0 %collective-permute-done.10.refs_1_ = bf16[64,1792]{1,0:T(8,128)(2,1)S(1)} collective-permute-done((bf16[64,1792]{1,0:T(8,128)(2,1)S(1)}, bf16[64,1792]{1,0:T(8,128)(2,1)S(1)}, u32[]{:S(2)}, u32[]{:S(2)}) %collective-permute-start.10) | collective-permute-done | bytes 229408 | tf_op jit(solution)/shard_map/ppermute | solution.py:20
  188.1 3.1 copy-done.4
  191.2 5.5 %shard_map.114 = (f32[256,256]{1,0:T(8,128)S(1)}, bf16[256,256]{1,0:T(8,128)(2,1)S(1)}, bf16[256,256]{1,0:T(8,128)(2,1)S(1)}, bf16[256,256]{1,0:T(8,128)(2,1)S(1...) custom-call(s32[2]{0:T(128)S(1)} %pad_add_fusion.idx_ref, ...), custom_call_target="tpu_custom_call" | custom-call | flops 1879048192 | bytes 7340032 | tf_op jit(solution)/shard_map/pallas_call | solution.py:67
  196.7 10.6 %collective-permute-start.19 = (bf16[256,256]{1,0:T(8,128)(2,1)S(1)}, bf16[256,256]{1,0:T(8,128)(2,1)S(1)}, u32[]{:S(2)}, u32[]{:S(2)}) collective-permute-start(bf16[256,256]{1,0:T(8,128)(2,1)S(1)} %get-tuple-element.63), channel_id=1, source_target_pairs={{0,7},{1,0},{2,1},{3,2},{4,3},{5,4},{6,5},{7,6},{8,15},{9,8},{10,9... | collective-permute-start | bytes 393224 | tf_op jit(solution)/shard_map/ppermute | solution.py:20
  223.6 4.2 collective-permute-start.22
  232.2 2.7 collective-permute-start.26
  238.0 3.0 collective-permute-start.48
  244.0 3.1 copy-done
  247.1 5.8 %shard_map.115 = (f32[2,64,896]{2,1,0:T(8,128)S(1)}, bf16[2,64,896]{2,1,0:T(8,128)(2,1)S(1)}, bf16[2,64,896]{2,1,0:T(8,128)(2,1)S(1)}, bf16[2,64,896]{2,1,0:T(8,128)(2,1)S(1)}, bf16[32,2048]{1,0:T(8,128)(2,1)S(1)}) custom-call(s32[2]{0:T(128)S(1)} %pad_add_fusion.idx_ref, bf16[256,256]{1,0:T(8,128)(2,1)S(1)} %add_convert_fusion.3.refs_0_, ...), custom_call_target="tpu_custom_call" | custom-call | flops 1879048192 | bytes 7340032 | tf_op jit(solution)/shard_map/pallas_call | solution.py:67
  252.9 3.6 collective-permute-start.33
  262.5 3.0 collective-permute-done.51.refs_6_
  267.6 4.6 %shard_map.117 = (f32[64,896]{1,0:T(8,128)S(1)}, bf16[64,896]{1,0:T(8,128)(2,1)S(1)}, bf16[64,896]{1,0:T(8,128)(2,1)S(1)}, bf16[64,896]{1,0:T(8,128)(2,1)S(1)}, bf16[256,256]{1,0:T(8,128)(2,1)S(1)}) custom-call(s32[2]{0:T(128)S(1)} %pad_add_fusion.idx_ref, bf16[32,2048]{1,0:T(8,128)(2,1)S(1)} %bitcast.95, ...), custom_call_target="tpu_custom_call" | custom-call | flops 939524096 | bytes 3670016 | tf_op jit(solution)/shard_map/pallas_call | solution.py:67
  272.2 3.2 collective-permute-start.55
  279.0 4.0 collective-permute-done.54
  283.0 4.0 collective-permute-done.53
  287.8 2.8 collective-permute-start.58
  290.6 6.4 %collective-permute-done.56.refs_1_ = bf16[2,64,896]{2,1,0:T(8,128)(2,1)S(1)} collective-permute-done((bf16[2,64,896]{2,1,0:T(8,128)(2,1)S(1)}, bf16[2,64,896]{2,1,0:T(8,128)(2,1)S(1)}, u32[]{:S(2)}, u32[]{:S(2)}) %collective-permute-start.56) | collective-permute-done | bytes 229408 | tf_op jit(solution)/shard_map/ppermute | solution.py:20
  297.9 4.7 %shard_map.118 = (f32[256,256]{1,0:T(8,128)S(1)}, bf16[256,256]{1,0:T(8,128)(2,1)S(1)}, bf16[256,256]{1,0:T(8,128)(2,1)S(1)}, bf16[256,256]{1,0:T(8,128)(2,1)S(1...) custom-call(s32[2]{0:T(128)S(1)} %pad_add_fusion.idx_ref, ...), custom_call_target="tpu_custom_call" | custom-call | flops 1879048192 | bytes 7340032 | tf_op jit(solution)/shard_map/pallas_call | solution.py:67
  302.6 4.2 collective-permute-start.65
  311.8 3.2 collective-permute-start.60
  315.1 10.4 %collective-permute-start.59 = (bf16[256,256]{1,0:T(8,128)(2,1)S(1)}, bf16[256,256]{1,0:T(8,128)(2,1)S(1)}, u32[]{:S(2)}, u32[]{:S(2)}) collective-permute-start(bf16[256,256]{1,0:T(8,128)(2,1)S(1)} %get-tuple-element.83), channel_id=1, source_target_pairs={{0,1},{1,2},{2,3},{3,4},{4,5},{5,6},{6,7},{7,0},{8,9},{9,10},{10,1... | collective-permute-start | bytes 393224 | tf_op jit(solution)/shard_map/ppermute | solution.py:20
  325.5 6.1 %collective-permute-done.59 = bf16[256,256]{1,0:T(8,128)(2,1)S(1)} collective-permute-done((bf16[256,256]{1,0:T(8,128)(2,1)S(1)}, bf16[256,256]{1,0:T(8,128)(2,1)S(1)}, u32[]{:S(2)}, u32[]{:S(2)}) %collective-permute-start.59) | collective-permute-done | bytes 131104 | tf_op jit(solution)/shard_map/ppermute | solution.py:20
  334.4 2.9 collective-permute-start.68
  342.1 3.2 collective-permute-start.72
  348.3 4.7 %shard_map.119 = (f32[64,1792]{1,0:T(8,128)S(1)}, bf16[64,1792]{1,0:T(8,128)(2,1)S(1)}, bf16[64,1792]{1,0:T(8,128)(2,1)S(1)}, bf16[64,1792]{1,0:T(8,128)(2,1)S(1)}) custom-call(s32[2]{0:T(128)S(1)} %pad_add_fusion.idx_ref, bf16[256,256]{1,0:T(8,128)(2,1)S(1)} %add_convert_fusion.1.refs_0_, bf16[256,256]{1,0:T(8,128)(2,1)S(1)} %collective-permute-done.66.refs_1_, ...), custom_call_target="tpu_custom_call" | custom-call | flops 1879048192 | bytes 7340032 | tf_op jit(solution)/shard_map/pallas_call | solution.py:67
  356.6 7.0 %collective-permute-done.75 = bf16[64,1792]{1,0:T(8,128)(2,1)S(1)} collective-permute-done((bf16[64,1792]{1,0:T(8,128)(2,1)S(1)}, bf16[64,1792]{1,0:T(8,128)(2,1)S(1)}, u32[]{:S(2)}, u32[]{:S(2)}) %collective-permute-start.75) | collective-permute-done | bytes 229408 | tf_op jit(solution)/shard_map/ppermute | solution.py:20
  365.7 3.9 collective-permute-done.73
  376.2 10.9 %collective-permute-done.34.refs_1_ = bf16[64,896]{1,0:T(8,128)(2,1)S(1)} collective-permute-done((bf16[64,896]{1,0:T(8,128)(2,1)S(1)}, bf16[64,896]{1,0:T(8,128)(2,1)S(1)}, u32[]{:S(2)}, u32[]{:S(2)}) %collective-permute-start.34) | collective-permute-done | bytes 114720 | tf_op jit(solution)/shard_map/ppermute | solution.py:20
  387.1 4.8 %collective-permute-done.36.refs_3_ = bf16[64,896]{1,0:T(8,128)(2,1)S(1)} collective-permute-done((bf16[64,896]{1,0:T(8,128)(2,1)S(1)}, bf16[64,896]{1,0:T(8,128)(2,1)S(1)}, u32[]{:S(2)}, u32[]{:S(2)}) %collective-permute-start.36) | collective-permute-done | bytes 114720 | tf_op jit(solution)/shard_map/ppermute | solution.py:20
  391.9 3.3 shard_map.116
  401.8 6.5 %shard_map.120 = (f32[256,256]{1,0:T(8,128)S(1)}, bf16[256,256]{1,0:T(8,128)(2,1)S(1)}, bf16[256,256]{1,0:T(8,128)(2,1)S(1)}, bf16[256,256]{1,0:T(8,128)(2,1)S(1...) custom-call(s32[2]{0:T(128)S(1)} %pad_add_fusion.idx_ref, ...), custom_call_target="tpu_custom_call" | custom-call | flops 3758096384 | bytes 14680064 | tf_op jit(solution)/shard_map/pallas_call | solution.py:67
  408.3 3.3 collective-permute-start.40
  411.6 4.1 collective-permute-start.85
  420.3 3.1 collective-permute-start.80
  (198 shorter events, 110.0 us)
Async XLA Ops:
  7.2 236.8 %all-gather.5.cloned.1.call-start = ((), (), s32[]{:S(2)}) async-start(), calls=%async_computation | async-start | bytes 9175040 | tf_op jit(solution)/shard_map/all_gather | solution.py:437
  8.5 10.1 %collective-permute-start.30 = (bf16[256,896]{1,0:T(8,128)(2,1)S(1)}, bf16[256,896]{1,0:T(8,128)(2,1)S(1)}, u32[]{:S(2)}, u32[]{:S(2)}) collective-permute-start(bf16[256,896]{1,0:T(8,128)(2,1)S(1)} %get-tuple-element.111), channel_id=1, source_target_pairs={{0,1},{1,0},{2,9},{3,8},{4,17},{5,16},{6,25},{7,24},{8,3},{9,2},{1... | collective-permute-start | bytes 1376264 | tf_op jit(solution)/shard_map/ppermute | solution.py:404
  11.1 17.4 %collective-permute-start.28 = (bf16[256,896]{1,0:T(8,128)(2,1)S(1)}, bf16[256,896]{1,0:T(8,128)(2,1)S(1)}, u32[]{:S(2)}, u32[]{:S(2)}) collective-permute-start(bf16[256,896]{1,0:T(8,128)(2,1)S(1)} %get-tuple-element.109), channel_id=1, source_target_pairs={{0,1},{1,0},{2,9},{3,8},{4,17},{5,16},{6,25},{7,24},{8,3},{9,2},{1... | collective-permute-start | bytes 1376264 | tf_op jit(solution)/shard_map/ppermute | solution.py:404
  11.5 17.0 %collective-permute-start.27 = (bf16[256,896]{1,0:T(8,128)(2,1)S(1)}, bf16[256,896]{1,0:T(8,128)(2,1)S(1)}, u32[]{:S(2)}, u32[]{:S(2)}) collective-permute-start(bf16[256,896]{1,0:T(8,128)(2,1)S(1)} %get-tuple-element.108), channel_id=1, source_target_pairs={{0,0},{1,1},{2,8},{3,9},{4,16},{5,17},{6,24},{7,25},{8,2},{9,3},{1... | collective-permute-start | bytes 1376264 | tf_op jit(solution)/shard_map/ppermute | solution.py:404
  30.1 235.5 %all-gather.7.cloned.1.call-start = ((), (), s32[]{:S(2)}) async-start(), calls=%async_computation.1 | async-start | bytes 4587520 | tf_op jit(solution)/shard_map/all_gather | solution.py:439
  40.9 86.8 %collective-permute-start = (bf16[256,256]{1,0:T(8,128)(2,1)S(1)}, bf16[256,256]{1,0:T(8,128)(2,1)S(1)}, u32[]{:S(2)}, u32[]{:S(2)}) collective-permute-start(bf16[256,256]{1,0:T(8,128)(2,1)S(1)} %bitcast.80), channel_id=1, source_target_pairs={{0,1},{1,2},{2,3},{3,4},{4,5},{5,6},{6,7},{7,0},{8,9},{9,10},{10,1... | collective-permute-start | bytes 393224 | tf_op jit(solution)/shard_map/ppermute | solution.py:20
  42.9 86.3 %collective-permute-start.1 = (bf16[256,256]{1,0:T(8,128)(2,1)S(1)}, bf16[256,256]{1,0:T(8,128)(2,1)S(1)}, u32[]{:S(2)}, u32[]{:S(2)}) collective-permute-start(bf16[256,256]{1,0:T(8,128)(2,1)S(1)} %bitcast.81), channel_id=1, source_target_pairs={{0,2},{1,3},{2,4},{3,5},{4,6},{5,7},{6,0},{7,1},{8,10},{9,11},{10,... | collective-permute-start | bytes 393224 | tf_op jit(solution)/shard_map/ppermute | solution.py:20
  55.0 75.9 %collective-permute-start.2 = (bf16[256,256]{1,0:T(8,128)(2,1)S(1)}, bf16[256,256]{1,0:T(8,128)(2,1)S(1)}, u32[]{:S(2)}, u32[]{:S(2)}) collective-permute-start(bf16[256,256]{1,0:T(8,128)(2,1)S(1)} %bitcast.82), channel_id=1, source_target_pairs={{0,3},{1,4},{2,5},{3,6},{4,7},{5,0},{6,1},{7,2},{8,11},{9,12},{10,... | collective-permute-start | bytes 393224 | tf_op jit(solution)/shard_map/ppermute | solution.py:20
  129.2 11.0 %collective-permute-start.6 = (bf16[256,256]{1,0:T(8,128)(2,1)S(1)}, bf16[256,256]{1,0:T(8,128)(2,1)S(1)}, u32[]{:S(2)}, u32[]{:S(2)}) collective-permute-start(bf16[256,256]{1,0:T(8,128)(2,1)S(1)} %bitcast.86), channel_id=1, source_target_pairs={{0,7},{1,0},{2,1},{3,2},{4,3},{5,4},{6,5},{7,6},{8,15},{9,8},{10,9... | collective-permute-start | bytes 393224 | tf_op jit(solution)/shard_map/ppermute | solution.py:20
  154.5 17.6 %collective-permute-start.9 = (bf16[2,64,1792]{2,1,0:T(8,128)(2,1)S(1)}, bf16[2,64,1792]{2,1,0:T(8,128)(2,1)S(1)}, u32[]{:S(2)}, u32[]{:S(2)}) collective-permute-start(bf16[2,64,1792]{2,1,0:T(8,128)(2,1)S(1)} %get-tuple-element.55), channel_id=1, source_target_pairs={{0,96},{32,0},{64,32},{96,64},{1,97},{33,1},{65,33},{97,65},{2,98}... | collective-permute-start | bytes 1376264 | tf_op jit(solution)/shard_map/ppermute | solution.py:20
  159.4 12.6 %collective-permute-start.8 = (bf16[2,64,1792]{2,1,0:T(8,128)(2,1)S(1)}, bf16[2,64,1792]{2,1,0:T(8,128)(2,1)}, u32[]{:S(2)}, u32[]{:S(2)}) collective-permute-start(bf16[2,64,1792]{2,1,0:T(8,128)(2,1)S(1)} %get-tuple-element.54), channel_id=1, source_target_pairs={{0,64},{32,96},{64,0},{96,32},{1,65},{33,97},{65,1},{97,33},{2,66}... | collective-permute-start | bytes 1376264 | tf_op jit(solution)/shard_map/ppermute | solution.py:20
  159.4 16.2 %collective-permute-start.7 = (bf16[2,64,1792]{2,1,0:T(8,128)(2,1)S(1)}, bf16[2,64,1792]{2,1,0:T(8,128)(2,1)}, u32[]{:S(2)}, u32[]{:S(2)}) collective-permute-start(bf16[2,64,1792]{2,1,0:T(8,128)(2,1)S(1)} %get-tuple-element.53), channel_id=1, source_target_pairs={{0,32},{32,64},{64,96},{96,0},{1,33},{33,65},{65,97},{97,1},{2,34}... | collective-permute-start | bytes 1376264 | tf_op jit(solution)/shard_map/ppermute | solution.py:20
  177.2 10.3 %collective-permute-start.10 = (bf16[64,1792]{1,0:T(8,128)(2,1)S(1)}, bf16[64,1792]{1,0:T(8,128)(2,1)S(1)}, u32[]{:S(2)}, u32[]{:S(2)}) collective-permute-start(bf16[64,1792]{1,0:T(8,128)(2,1)S(1)} %multiply_convert_fusion.2.refs_0_), channel_id=1, source_target_pairs={{0,32},{32,64},{64,96},{96,0},{1,33},{33,65},{65,97},{97,1},{2,34}... | collective-permute-start | bytes 688136 | tf_op jit(solution)/shard_map/ppermute | solution.py:20
  177.2 10.2 %collective-permute-start.11 = (bf16[64,1792]{1,0:T(8,128)(2,1)S(1)}, bf16[64,1792]{1,0:T(8,128)(2,1)S(1)}, u32[]{:S(2)}, u32[]{:S(2)}) collective-permute-start(bf16[64,1792]{1,0:T(8,128)(2,1)S(1)} %multiply_convert_fusion.2.refs_0_), channel_id=1, source_target_pairs={{0,64},{32,96},{64,0},{96,32},{1,65},{33,97},{65,1},{97,33},{2,66}... | collective-permute-start | bytes 688136 | tf_op jit(solution)/shard_map/ppermute | solution.py:20
  196.7 14.6 %collective-permute-start.19 = (bf16[256,256]{1,0:T(8,128)(2,1)S(1)}, bf16[256,256]{1,0:T(8,128)(2,1)S(1)}, u32[]{:S(2)}, u32[]{:S(2)}) collective-permute-start(bf16[256,256]{1,0:T(8,128)(2,1)S(1)} %get-tuple-element.63), channel_id=1, source_target_pairs={{0,7},{1,0},{2,1},{3,2},{4,3},{5,4},{6,5},{7,6},{8,15},{9,8},{10,9... | collective-permute-start | bytes 393224 | tf_op jit(solution)/shard_map/ppermute | solution.py:20
  211.2 9.8 %collective-permute-start.14 = (bf16[256,256]{1,0:T(8,128)(2,1)S(1)}, bf16[256,256]{1,0:T(8,128)(2,1)S(1)}, u32[]{:S(2)}, u32[]{:S(2)}) collective-permute-start(bf16[256,256]{1,0:T(8,128)(2,1)S(1)} %get-tuple-element.58), channel_id=1, source_target_pairs={{0,2},{1,3},{2,4},{3,5},{4,6},{5,7},{6,0},{7,1},{8,10},{9,11},{10,... | collective-permute-start | bytes 393224 | tf_op jit(solution)/shard_map/ppermute | solution.py:20
  223.6 11.4 %collective-permute-start.22 = (bf16[256,256]{1,0:T(8,128)(2,1)S(1)}, bf16[256,256]{1,0:T(8,128)(2,1)S(1)}, u32[]{:S(2)}, u32[]{:S(2)}) collective-permute-start(bf16[256,256]{1,0:T(8,128)(2,1)S(1)} %add_convert_fusion.3.refs_0_), channel_id=1, source_target_pairs={{0,3},{1,4},{2,5},{3,6},{4,7},{5,0},{6,1},{7,2},{8,11},{9,12},{10,... | collective-permute-start | bytes 393224 | tf_op jit(solution)/shard_map/ppermute | solution.py:20
  227.8 10.2 %collective-permute-start.24 = (bf16[256,256]{1,0:T(8,128)(2,1)S(1)}, bf16[256,256]{1,0:T(8,128)(2,1)S(1)}, u32[]{:S(2)}, u32[]{:S(2)}) collective-permute-start(bf16[256,256]{1,0:T(8,128)(2,1)S(1)} %add_convert_fusion.3.refs_0_), channel_id=1, source_target_pairs={{0,5},{1,6},{2,7},{3,0},{4,1},{5,2},{6,3},{7,4},{8,13},{9,14},{10,... | collective-permute-start | bytes 393224 | tf_op jit(solution)/shard_map/ppermute | solution.py:20
  232.2 10.6 %collective-permute-start.26 = (bf16[256,256]{1,0:T(8,128)(2,1)S(1)}, bf16[256,256]{1,0:T(8,128)(2,1)S(1)}, u32[]{:S(2)}, u32[]{:S(2)}) collective-permute-start(bf16[256,256]{1,0:T(8,128)(2,1)S(1)} %add_convert_fusion.3.refs_0_), channel_id=1, source_target_pairs={{0,7},{1,0},{2,1},{3,2},{4,3},{5,4},{6,5},{7,6},{8,15},{9,8},{10,9... | collective-permute-start | bytes 393224 | tf_op jit(solution)/shard_map/ppermute | solution.py:20
  235.0 18.0 %collective-permute-start.46 = (bf16[32,2048]{1,0:T(8,128)(2,1)S(1)}, bf16[32,2048]{1,0:T(8,128)(2,1)S(1)}, u32[]{:S(2)}, u32[]{:S(2)}) collective-permute-start(bf16[32,2048]{1,0:T(8,128)(2,1)S(1)} %bitcast.88), channel_id=1, source_target_pairs={{0,1},{1,2},{2,3},{3,4},{4,5},{5,6},{6,7},{7,0},{8,9},{9,10},{10,1... | collective-permute-start | bytes 393224 | tf_op jit(solution)/shard_map/ppermute | solution.py:20
  235.9 20.6 %collective-permute-start.47 = (bf16[32,2048]{1,0:T(8,128)(2,1)S(1)}, bf16[32,2048]{1,0:T(8,128)(2,1)S(1)}, u32[]{:S(2)}, u32[]{:S(2)}) collective-permute-start(bf16[32,2048]{1,0:T(8,128)(2,1)S(1)} %bitcast.89), channel_id=1, source_target_pairs={{0,2},{1,3},{2,4},{3,5},{4,6},{5,7},{6,0},{7,1},{8,10},{9,11},{10,... | collective-permute-start | bytes 393224 | tf_op jit(solution)/shard_map/ppermute | solution.py:20
  238.0 21.0 %collective-permute-start.48 = (bf16[32,2048]{1,0:T(8,128)(2,1)S(1)}, bf16[32,2048]{1,0:T(8,128)(2,1)S(1)}, u32[]{:S(2)}, u32[]{:S(2)}) collective-permute-start(bf16[32,2048]{1,0:T(8,128)(2,1)S(1)} %bitcast.90), channel_id=1, source_target_pairs={{0,3},{1,4},{2,5},{3,6},{4,7},{5,0},{6,1},{7,2},{8,11},{9,12},{10,... | collective-permute-start | bytes 393224 | tf_op jit(solution)/shard_map/ppermute | solution.py:20
  241.0 18.0 %collective-permute-start.49 = (bf16[32,2048]{1,0:T(8,128)(2,1)S(1)}, bf16[32,2048]{1,0:T(8,128)(2,1)S(1)}, u32[]{:S(2)}, u32[]{:S(2)}) collective-permute-start(bf16[32,2048]{1,0:T(8,128)(2,1)S(1)} %bitcast.91), channel_id=1, source_target_pairs={{0,4},{1,5},{2,6},{3,7},{4,0},{5,1},{6,2},{7,3},{8,12},{9,13},{10,... | collective-permute-start | bytes 393224 | tf_op jit(solution)/shard_map/ppermute | solution.py:20
  242.8 16.6 %collective-permute-start.50 = (bf16[32,2048]{1,0:T(8,128)(2,1)S(1)}, bf16[32,2048]{1,0:T(8,128)(2,1)S(1)}, u32[]{:S(2)}, u32[]{:S(2)}) collective-permute-start(bf16[32,2048]{1,0:T(8,128)(2,1)S(1)} %bitcast.92), channel_id=1, source_target_pairs={{0,5},{1,6},{2,7},{3,0},{4,1},{5,2},{6,3},{7,4},{8,13},{9,14},{10,... | collective-permute-start | bytes 393224 | tf_op jit(solution)/shard_map/ppermute | solution.py:20
  252.9 23.5 %collective-permute-start.33 = (bf16[2,64,896]{2,1,0:T(8,128)(2,1)S(1)}, bf16[2,64,896]{2,1,0:T(8,128)(2,1)S(1)}, u32[]{:S(2)}, u32[]{:S(2)}) collective-permute-start(bf16[2,64,896]{2,1,0:T(8,128)(2,1)S(1)} %get-tuple-element.68), channel_id=1, source_target_pairs={{0,96},{32,0},{64,32},{96,64},{1,97},{33,1},{65,33},{97,65},{2,98}... | collective-permute-start | bytes 688136 | tf_op jit(solution)/shard_map/ppermute | solution.py:20
  256.6 19.9 %collective-permute-start.32 = (bf16[2,64,896]{2,1,0:T(8,128)(2,1)S(1)}, bf16[2,64,896]{2,1,0:T(8,128)(2,1)S(1)}, u32[]{:S(2)}, u32[]{:S(2)}) collective-permute-start(bf16[2,64,896]{2,1,0:T(8,128)(2,1)S(1)} %get-tuple-element.67), channel_id=1, source_target_pairs={{0,64},{32,96},{64,0},{96,32},{1,65},{33,97},{65,1},{97,33},{2,66}... | collective-permute-start | bytes 688136 | tf_op jit(solution)/shard_map/ppermute | solution.py:20
  259.0 17.4 %collective-permute-start.31 = (bf16[2,64,896]{2,1,0:T(8,128)(2,1)S(1)}, bf16[2,64,896]{2,1,0:T(8,128)(2,1)S(1)}, u32[]{:S(2)}, u32[]{:S(2)}) collective-permute-start(bf16[2,64,896]{2,1,0:T(8,128)(2,1)S(1)} %get-tuple-element.66), channel_id=1, source_target_pairs={{0,32},{32,64},{64,96},{96,0},{1,33},{33,65},{65,97},{97,1},{2,34}... | collective-permute-start | bytes 688136 | tf_op jit(solution)/shard_map/ppermute | solution.py:20
  276.5 10.6 %collective-permute-start.53 = (bf16[64,896]{1,0:T(8,128)(2,1)S(1)}, bf16[64,896]{1,0:T(8,128)(2,1)S(1)}, u32[]{:S(2)}, u32[]{:S(2)}) collective-permute-start(bf16[64,896]{1,0:T(8,128)(2,1)S(1)} %get-tuple-element.79), channel_id=1, source_target_pairs={{0,32},{32,64},{64,96},{96,0},{1,33},{33,65},{65,97},{97,1},{2,34}... | collective-permute-start | bytes 344072 | tf_op jit(solution)/shard_map/ppermute | solution.py:20
  287.8 10.2 %collective-permute-start.58 = (bf16[2,64,896]{2,1,0:T(8,128)(2,1)S(1)}, bf16[2,64,896]{2,1,0:T(8,128)(2,1)S(1)}, u32[]{:S(2)}, u32[]{:S(2)}) collective-permute-start(bf16[2,64,896]{2,1,0:T(8,128)(2,1)S(1)} %pad_maximum_fusion.3.refs_0_), channel_id=1, source_target_pairs={{0,96},{32,0},{64,32},{96,64},{1,97},{33,1},{65,33},{97,65},{2,98}... | collective-permute-start | bytes 688136 | tf_op jit(solution)/shard_map/ppermute | solution.py:20
  307.3 18.2 %collective-permute-start.63 = (bf16[256,256]{1,0:T(8,128)(2,1)S(1)}, bf16[256,256]{1,0:T(8,128)(2,1)S(1)}, u32[]{:S(2)}, u32[]{:S(2)}) collective-permute-start(bf16[256,256]{1,0:T(8,128)(2,1)S(1)} %get-tuple-element.87), channel_id=1, source_target_pairs={{0,5},{1,6},{2,7},{3,0},{4,1},{5,2},{6,3},{7,4},{8,13},{9,14},{10,... | collective-permute-start | bytes 393224 | tf_op jit(solution)/shard_map/ppermute | solution.py:20
  309.0 16.5 %collective-permute-start.62 = (bf16[256,256]{1,0:T(8,128)(2,1)S(1)}, bf16[256,256]{1,0:T(8,128)(2,1)S(1)}, u32[]{:S(2)}, u32[]{:S(2)}) collective-permute-start(bf16[256,256]{1,0:T(8,128)(2,1)S(1)} %get-tuple-element.86), channel_id=1, source_target_pairs={{0,4},{1,5},{2,6},{3,7},{4,0},{5,1},{6,2},{7,3},{8,12},{9,13},{10,... | collective-permute-start | bytes 393224 | tf_op jit(solution)/shard_map/ppermute | solution.py:20
  309.2 16.2 %collective-permute-start.61 = (bf16[256,256]{1,0:T(8,128)(2,1)S(1)}, bf16[256,256]{1,0:T(8,128)(2,1)S(1)}, u32[]{:S(2)}, u32[]{:S(2)}) collective-permute-start(bf16[256,256]{1,0:T(8,128)(2,1)S(1)} %get-tuple-element.85), channel_id=1, source_target_pairs={{0,3},{1,4},{2,5},{3,6},{4,7},{5,0},{6,1},{7,2},{8,11},{9,12},{10,... | collective-permute-start | bytes 393224 | tf_op jit(solution)/shard_map/ppermute | solution.py:20
  311.8 13.6 %collective-permute-start.60 = (bf16[256,256]{1,0:T(8,128)(2,1)S(1)}, bf16[256,256]{1,0:T(8,128)(2,1)S(1)}, u32[]{:S(2)}, u32[]{:S(2)}) collective-permute-start(bf16[256,256]{1,0:T(8,128)(2,1)S(1)} %get-tuple-element.84), channel_id=1, source_target_pairs={{0,2},{1,3},{2,4},{3,5},{4,6},{5,7},{6,0},{7,1},{8,10},{9,11},{10,... | collective-permute-start | bytes 393224 | tf_op jit(solution)/shard_map/ppermute | solution.py:20
  315.1 16.4 %collective-permute-start.59 = (bf16[256,256]{1,0:T(8,128)(2,1)S(1)}, bf16[256,256]{1,0:T(8,128)(2,1)S(1)}, u32[]{:S(2)}, u32[]{:S(2)}) collective-permute-start(bf16[256,256]{1,0:T(8,128)(2,1)S(1)} %get-tuple-element.83), channel_id=1, source_target_pairs={{0,1},{1,2},{2,3},{3,4},{4,5},{5,6},{6,7},{7,0},{8,9},{9,10},{10,1... | collective-permute-start | bytes 393224 | tf_op jit(solution)/shard_map/ppermute | solution.py:20
  334.4 10.8 %collective-permute-start.68 = (bf16[256,256]{1,0:T(8,128)(2,1)S(1)}, bf16[256,256]{1,0:T(8,128)(2,1)S(1)}, u32[]{:S(2)}, u32[]{:S(2)}) collective-permute-start(bf16[256,256]{1,0:T(8,128)(2,1)S(1)} %add_convert_fusion.1.refs_0_), channel_id=1, source_target_pairs={{0,3},{1,4},{2,5},{3,6},{4,7},{5,0},{6,1},{7,2},{8,11},{9,12},{10,... | collective-permute-start | bytes 393224 | tf_op jit(solution)/shard_map/ppermute | solution.py:20
  353.0 10.5 %collective-permute-start.75 = (bf16[64,1792]{1,0:T(8,128)(2,1)S(1)}, bf16[64,1792]{1,0:T(8,128)(2,1)S(1)}, u32[]{:S(2)}, u32[]{:S(2)}) collective-permute-start(bf16[64,1792]{1,0:T(8,128)(2,1)S(1)} %get-tuple-element.93), channel_id=1, source_target_pairs={{0,96},{32,0},{64,32},{96,64},{1,97},{33,1},{65,33},{97,65},{2,98}... | collective-permute-start | bytes 688136 | tf_op jit(solution)/shard_map/ppermute | solution.py:20
  355.6 10.1 %collective-permute-start.74 = (bf16[64,1792]{1,0:T(8,128)(2,1)S(1)}, bf16[64,1792]{1,0:T(8,128)(2,1)S(1)}, u32[]{:S(2)}, u32[]{:S(2)}) collective-permute-start(bf16[64,1792]{1,0:T(8,128)(2,1)S(1)} %get-tuple-element.92), channel_id=1, source_target_pairs={{0,64},{32,96},{64,0},{96,32},{1,65},{33,97},{65,1},{97,33},{2,66}... | collective-permute-start | bytes 688136 | tf_op jit(solution)/shard_map/ppermute | solution.py:20
  355.6 13.9 %collective-permute-start.73 = (bf16[64,1792]{1,0:T(8,128)(2,1)S(1)}, bf16[64,1792]{1,0:T(8,128)(2,1)S(1)}, u32[]{:S(2)}, u32[]{:S(2)}) collective-permute-start(bf16[64,1792]{1,0:T(8,128)(2,1)S(1)} %get-tuple-element.91), channel_id=1, source_target_pairs={{0,32},{32,64},{64,96},{96,0},{1,33},{33,65},{65,97},{97,1},{2,34}... | collective-permute-start | bytes 688136 | tf_op jit(solution)/shard_map/ppermute | solution.py:20
  369.9 27.8 %collective-permute-start.76 = (bf16[2,64,1792]{2,1,0:T(8,128)(2,1)S(1)}, bf16[2,64,1792]{2,1,0:T(8,128)(2,1)S(1)}, u32[]{:S(2)}, u32[]{:S(2)}) collective-permute-start(bf16[2,64,1792]{2,1,0:T(8,128)(2,1)S(1)} %pad_maximum_fusion.2.refs_0_), channel_id=1, source_target_pairs={{0,32},{32,64},{64,96},{96,0},{1,33},{33,65},{65,97},{97,1},{2,34}... | collective-permute-start | bytes 1376264 | tf_op jit(solution)/shard_map/ppermute | solution.py:20
  370.0 28.9 %collective-permute-start.77 = (bf16[2,64,1792]{2,1,0:T(8,128)(2,1)S(1)}, bf16[2,64,1792]{2,1,0:T(8,128)(2,1)S(1)}, u32[]{:S(2)}, u32[]{:S(2)}) collective-permute-start(bf16[2,64,1792]{2,1,0:T(8,128)(2,1)S(1)} %pad_maximum_fusion.2.refs_0_), channel_id=1, source_target_pairs={{0,64},{32,96},{64,0},{96,32},{1,65},{33,97},{65,1},{97,33},{2,66}... | collective-permute-start | bytes 1376264 | tf_op jit(solution)/shard_map/ppermute | solution.py:20
  371.5 28.6 %collective-permute-start.78 = (bf16[2,64,1792]{2,1,0:T(8,128)(2,1)S(1)}, bf16[2,64,1792]{2,1,0:T(8,128)(2,1)S(1)}, u32[]{:S(2)}, u32[]{:S(2)}) collective-permute-start(bf16[2,64,1792]{2,1,0:T(8,128)(2,1)S(1)} %pad_maximum_fusion.2.refs_0_), channel_id=1, source_target_pairs={{0,96},{32,0},{64,32},{96,64},{1,97},{33,1},{65,33},{97,65},{2,98}... | collective-permute-start | bytes 1376264 | tf_op jit(solution)/shard_map/ppermute | solution.py:20
  373.3 13.8 %collective-permute-start.34 = (bf16[64,896]{1,0:T(8,128)(2,1)S(1)}, bf16[64,896]{1,0:T(8,128)(2,1)S(1)}, u32[]{:S(2)}, u32[]{:S(2)}) collective-permute-start(bf16[64,896]{1,0:T(8,128)(2,1)S(1)} %get-tuple-element.112.refs_0_), channel_id=1, source_target_pairs={{0,32},{32,64},{64,96},{96,0},{1,33},{33,65},{65,97},{97,1},{2,34}... | collective-permute-start | bytes 344072 | tf_op jit(solution)/shard_map/ppermute | solution.py:20
  374.1 13.0 %collective-permute-start.35 = (bf16[64,896]{1,0:T(8,128)(2,1)S(1)}, bf16[64,896]{1,0:T(8,128)(2,1)S(1)}, u32[]{:S(2)}, u32[]{:S(2)}) collective-permute-start(bf16[64,896]{1,0:T(8,128)(2,1)S(1)} %get-tuple-element.112.refs_0_), channel_id=1, source_target_pairs={{0,64},{32,96},{64,0},{96,32},{1,65},{33,97},{65,1},{97,33},{2,66}... | collective-permute-start | bytes 344072 | tf_op jit(solution)/shard_map/ppermute | solution.py:20
  395.2 13.1 %collective-permute-start.45 = (bf16[32,2048]{1,0:T(8,128)(2,1)S(1)}, bf16[32,2048]{1,0:T(8,128)(2,1)S(1)}, u32[]{:S(2)}, u32[]{:S(2)}) collective-permute-start(bf16[32,2048]{1,0:T(8,128)(2,1)S(1)} %get-tuple-element.76), channel_id=1, source_target_pairs={{0,7},{1,0},{2,1},{3,2},{4,3},{5,4},{6,5},{7,6},{8,15},{9,8},{10,9... | collective-permute-start | bytes 393224 | tf_op jit(solution)/shard_map/ppermute | solution.py:20
  397.7 13.9 %collective-permute-start.44 = (bf16[32,2048]{1,0:T(8,128)(2,1)S(1)}, bf16[32,2048]{1,0:T(8,128)(2,1)S(1)}, u32[]{:S(2)}, u32[]{:S(2)}) collective-permute-start(bf16[32,2048]{1,0:T(8,128)(2,1)S(1)} %get-tuple-element.75), channel_id=1, source_target_pairs={{0,6},{1,7},{2,0},{3,1},{4,2},{5,3},{6,4},{7,5},{8,14},{9,15},{10,... | collective-permute-start | bytes 393224 | tf_op jit(solution)/shard_map/ppermute | solution.py:20
  397.7 13.9 %collective-permute-start.43 = (bf16[32,2048]{1,0:T(8,128)(2,1)S(1)}, bf16[32,2048]{1,0:T(8,128)(2,1)S(1)}, u32[]{:S(2)}, u32[]{:S(2)}) collective-permute-start(bf16[32,2048]{1,0:T(8,128)(2,1)S(1)} %get-tuple-element.74), channel_id=1, source_target_pairs={{0,5},{1,6},{2,7},{3,0},{4,1},{5,2},{6,3},{7,4},{8,13},{9,14},{10,... | collective-permute-start | bytes 393224 | tf_op jit(solution)/shard_map/ppermute | solution.py:20
  398.9 16.9 %collective-permute-start.42 = (bf16[32,2048]{1,0:T(8,128)(2,1)S(1)}, bf16[32,2048]{1,0:T(8,128)(2,1)S(1)}, u32[]{:S(2)}, u32[]{:S(2)}) collective-permute-start(bf16[32,2048]{1,0:T(8,128)(2,1)S(1)} %get-tuple-element.73), channel_id=1, source_target_pairs={{0,4},{1,5},{2,6},{3,7},{4,0},{5,1},{6,2},{7,3},{8,12},{9,13},{10,... | collective-permute-start | bytes 393224 | tf_op jit(solution)/shard_map/ppermute | solution.py:20
  400.1 15.7 %collective-permute-start.41 = (bf16[32,2048]{1,0:T(8,128)(2,1)S(1)}, bf16[32,2048]{1,0:T(8,128)(2,1)S(1)}, u32[]{:S(2)}, u32[]{:S(2)}) collective-permute-start(bf16[32,2048]{1,0:T(8,128)(2,1)S(1)} %get-tuple-element.72), channel_id=1, source_target_pairs={{0,3},{1,4},{2,5},{3,6},{4,7},{5,0},{6,1},{7,2},{8,11},{9,12},{10,... | collective-permute-start | bytes 393224 | tf_op jit(solution)/shard_map/ppermute | solution.py:20
  (59 other events, 991.8 us)
Sparse Core Ops, SparseCore 0:
  30.2 82.5 all-gather.4
  114.5 45.3 all-gather.6

commit v2 on v1

v2 whole, which is shorter than its diff:
```python
import jax
import jax.numpy as jnp
from jax import lax
from jax.experimental import pallas as pl
from jax.experimental.pallas import tpu as pltpu
from jax.sharding import PartitionSpec as P

BF = jnp.bfloat16
F32 = jnp.float32
VMEM = 8 << 20
NT = (((1,), (1,)), ((), ()))


def ring(n, shift):
    return [(i, (i + shift) % n) for i in range(n)]


def send(parts, axis, n):
    return [lax.ppermute(p, axis, ring(n, r)) for r, p in zip(range(1, n), parts)]


def spread(own, axis, n):
    return [own] + send([own] * (n - 1), axis, n)


VM = pl.BlockSpec(memory_space=pltpu.VMEM)
SM = pl.BlockSpec(memory_space=pltpu.SMEM)


def fill_features(scratch, refs, t, mix, slot):
    width = refs[0].shape[1]
    for k, ref in enumerate(refs):
        owner = lax.rem(t - k + 8, 8)
        at = pl.multiple_of(slot(owner, mix) * width, width)
        scratch[:, pl.ds(at, width)] = ref[...]


def fill_rows(scratch, refs, me, n):
    rows = refs[0].shape[-2]
    for k, ref in enumerate(refs):
        at = pl.multiple_of(lax.rem(me - k + n, n) * rows, rows)
        if len(ref.shape) == 3:
            for g in range(ref.shape[0]):
                scratch[g, pl.ds(at, rows), :] = ref[g]
        else:
            scratch[pl.ds(at, rows), :] = ref[...]


def plain_slot(owner, mix):
    return owner


def narrow_slot(owner, mix):
    return owner ^ mix


def call(kernel, idx, operands, outs, scratch, flops, moved):
    return pl.pallas_call(
        kernel,
        in_specs=[SM] + [VM] * len(operands),
        out_specs=[VM] * len(outs),
        out_shape=[pltpu.VMEM(shape, kind) for shape, kind in outs],
        scratch_shapes=scratch,
        compiler_params=pltpu.CompilerParams(vmem_limit_bytes=VMEM),
        cost_estimate=pl.CostEstimate(flops=flops, bytes_accessed=moved, transcendentals=0),
    )(idx, *operands)


def into_vmem(*weights):
    n = len(weights)

    def kernel(*refs):
        copies = [
            pltpu.make_async_copy(refs[i], refs[n + i], refs[2 * n].at[i]) for i in range(n)
        ]
        for c in copies:
            c.start()
        for c in copies:
            c.wait()

    moved = sum(w.size * 2 for w in weights)
    return pl.pallas_call(
        kernel,
        in_specs=[pl.BlockSpec(memory_space=pltpu.HBM)] * n,
        out_specs=[VM] * n,
        out_shape=[pltpu.VMEM(w.shape, w.dtype) for w in weights],
        scratch_shapes=[pltpu.SemaphoreType.DMA((n,))],
        compiler_params=pltpu.CompilerParams(vmem_limit_bytes=1 << 20),
        cost_estimate=pl.CostEstimate(flops=0, bytes_accessed=2 * moved, transcendentals=0),
    )(*weights)


def gate_up(idx, chunks, weights, narrow):
    tokens, width = chunks[0].shape
    feats = 8 * width
    units = weights[0].shape[-1]
    block = 256
    rows = tokens // 4
    mid_rows = tokens // 8
    n_w = len(weights)

    def kernel(idx_ref, *refs):
        xs, ws = refs[:8], refs[8 : 8 + n_w]
        outs = refs[8 + n_w : 12 + n_w]
        mid, lhs, val = refs[12 + n_w :]
        s, t, mix = idx_ref[0], idx_ref[1], idx_ref[2]
        fill_features(lhs, xs, t, mix, narrow_slot if narrow else plain_slot)
        if narrow:
            row = pl.multiple_of(t * mid_rows, mid_rows)
            for k, ref in enumerate(xs):
                owner = lax.rem(t - k + 8, 8)
                to = pl.multiple_of(owner * width, width)
                mid[:, pl.ds(to, width)] = ref[pl.ds(row, mid_rows), :]
        for g in range(2):
            for at in range(0, units, block):
                size = min(block, units - at)
                if narrow:
                    value = None
                    for j, w in enumerate(ws):
                        term = jnp.dot(
                            lhs[:, j * width : (j + 1) * width],
                            w[g, :, at : at + size],
                            preferred_element_type=F32,
                        )
                        value = term if value is None else value + term
                else:
                    value = jnp.dot(lhs[...], ws[g][:, at : at + size], preferred_element_type=F32)
                val[:, :size] = value
                for r, out in enumerate(outs):
                    row = pl.multiple_of(lax.rem(s + r, 4) * rows, rows)
                    out[g, :, at : at + size] = val[pl.ds(row, rows), :size].astype(out.dtype)

    res = call(
        kernel,
        idx,
        (*chunks, *weights),
        [((2, rows, units), F32)] + [((2, rows, units), BF)] * 3 + [((mid_rows, feats), BF)],
        [pltpu.VMEM((tokens, feats), BF), pltpu.VMEM((tokens, block), F32)],
        4 * tokens * feats * units,
        4 * feats * units,
    )
    return res[0], res[1:4], res[4]


def down_wide_part(idx, chunks, down_w):
    rows, units = chunks[0].shape
    tokens = 4 * rows
    feats = down_w.shape[1]
    width = feats // 8

    def kernel(idx_ref, *refs):
        hs, w, outs, lhs = refs[:4], refs[4], refs[5:13], refs[13]
        fill_rows(lhs, hs, idx_ref[0], 4)
        for k, out in enumerate(outs):
            at = pl.multiple_of(lax.rem(idx_ref[1] + k, 8) * width, width)
            out[...] = jnp.dot(
                lhs[...], w[:, pl.ds(at, width)], preferred_element_type=F32
            ).astype(out.dtype)

    res = call(
        kernel,
        idx,
        (*chunks, down_w),
        [((tokens, width), F32)] + [((tokens, width), BF)] * 7,
        [pltpu.VMEM((tokens, units), BF)],
        2 * tokens * feats * units,
        2 * feats * units,
    )
    return res[0], res[1:]


def down_narrow_part(idx, chunks, weights):
    rows, units = chunks[0].shape
    tokens = 4 * rows
    width = weights[0].shape[-1]
    feats = 8 * width
    mid_rows = tokens // 8

    def kernel(idx_ref, *refs):
        hs, ws, outs, lhs, acc = refs[:4], refs[4:12], refs[12:20], refs[20], refs[21]
        t, mix = idx_ref[1], idx_ref[2]
        fill_rows(lhs, hs, idx_ref[0], 4)
        for j, w in enumerate(ws):
            at = pl.multiple_of((mix ^ j) * width, width)
            acc[:, pl.ds(at, width)] = jnp.dot(lhs[...], w[...], preferred_element_type=F32)
        for k, out in enumerate(outs):
            row = pl.multiple_of(lax.rem(t + k, 8) * mid_rows, mid_rows)
            out[...] = acc[pl.ds(row, mid_rows), :].astype(out.dtype)

    res = call(
        kernel,
        idx,
        (*chunks, *weights),
        [((mid_rows, feats), F32)] + [((mid_rows, feats), BF)] * 7,
        [pltpu.VMEM((tokens, units), BF), pltpu.VMEM((tokens, feats), F32)],
        2 * tokens * feats * units,
        2 * feats * units,
    )
    return res[0], res[1:]


def hidden_grad_wide(idx, chunks, down_w):
    tokens, width = chunks[0].shape
    feats = 8 * width
    units = down_w.shape[0]
    block = 256
    rows = tokens // 4

    def kernel(idx_ref, *refs):
        xs, w, outs, lhs, val = refs[:8], refs[8], refs[9:13], refs[13], refs[14]
        s, t = idx_ref[0], idx_ref[1]
        fill_features(lhs, xs, t, 0, plain_slot)
        for at in range(0, units, block):
            val[...] = lax.dot_general(
                lhs[...], w[at : at + block, :], NT, preferred_element_type=F32
            )
            for r, out in enumerate(outs):
                row = pl.multiple_of(lax.rem(s + r, 4) * rows, rows)
                out[:, at : at + block] = val[pl.ds(row, rows), :].astype(out.dtype)

    res = call(
        kernel,
        idx,
        (*chunks, down_w),
        [((rows, units), F32)] + [((rows, units), BF)] * 3,
        [pltpu.VMEM((tokens, feats), BF), pltpu.VMEM((tokens, block), F32)],
        2 * tokens * feats * units,
        2 * feats * units,
    )
    return res[0], res[1:]


def hidden_grad_narrow(idx, chunks, weights):
    mid_rows, feats = chunks[0].shape
    tokens = 8 * mid_rows
    width = feats // 8
    units = weights[0].shape[0]
    block = 256
    rows = tokens // 4

    def kernel(idx_ref, *refs):
        xs, ws, outs = refs[:8], refs[8:16], refs[16:20]
        own, lhs, val = refs[20:]
        s, t, mix = idx_ref[0], idx_ref[1], idx_ref[2]
        fill_rows(lhs, xs, t, 8)
        own[...] = lhs[:, pl.ds(pl.multiple_of(t * width, width), width)]
        for at in range(0, units, block):
            size = min(block, units - at)
            total = None
            for j, w in enumerate(ws):
                left = lhs[:, pl.ds(pl.multiple_of((mix ^ j) * width, width), width)]
                term = lax.dot_general(
                    left, w[at : at + size, :], NT, preferred_element_type=F32
                )
                total = term if total is None else total + term
            val[:, :size] = total
            for r, out in enumerate(outs):
                row = pl.multiple_of(lax.rem(s + r, 4) * rows, rows)
                out[:, at : at + size] = val[pl.ds(row, rows), :size].astype(out.dtype)

    res = call(
        kernel,
        idx,
        (*chunks, *weights),
        [((rows, units), F32)] + [((rows, units), BF)] * 3 + [((tokens, width), BF)],
        [pltpu.VMEM((tokens, feats), BF), pltpu.VMEM((tokens, block), F32)],
        2 * tokens * feats * units,
        2 * feats * units,
    )
    return res[0], res[1:4], res[4]


def input_back_wide(idx, chunks, gate_w, up_w):
    _, rows, units = chunks[0].shape
    tokens = 4 * rows
    width = gate_w.shape[0] // 8
    feats = 8 * width

    def kernel(idx_ref, *refs):
        ps, g, u, outs, lhs = refs[:4], refs[4], refs[5], refs[6:14], refs[14]
        fill_rows(lhs, ps, idx_ref[0], 4)
        for k, out in enumerate(outs):
            at = pl.multiple_of(lax.rem(idx_ref[1] + k, 8) * width, width)
            value = lax.dot_general(
                lhs[0], g[pl.ds(at, width), :], NT, preferred_element_type=F32
            )
            value += lax.dot_general(
                lhs[1], u[pl.ds(at, width), :], NT, preferred_element_type=F32
            )
            out[...] = value.astype(out.dtype)

    res = call(
        kernel,
        idx,
        (*chunks, gate_w, up_w),
        [((tokens, width), F32)] + [((tokens, width), BF)] * 7,
        [pltpu.VMEM((2, tokens, units), BF)],
        4 * tokens * feats * units,
        4 * feats * units,
    )
    return res[0], res[1:]


def input_back_narrow(idx, chunks, weights):
    _, rows, units = chunks[0].shape
    tokens = 4 * rows
    width = weights[0].shape[1]
    feats = 8 * width

    def kernel(idx_ref, *refs):
        ps, ws, outs, lhs, acc = refs[:4], refs[4:12], refs[12:20], refs[20], refs[21]
        t, mix = idx_ref[1], idx_ref[2]
        fill_rows(lhs, ps, idx_ref[0], 4)
        for j, w in enumerate(ws):
            value = lax.dot_general(lhs[0], w[0], NT, preferred_element_type=F32)
            value += lax.dot_general(lhs[1], w[1], NT, preferred_element_type=F32)
            acc[mix ^ j] = value
        for k, out in enumerate(outs):
            out[...] = acc[lax.rem(t + k, 8)].astype(out.dtype)

    res = call(
        kernel,
        idx,
        (*chunks, *weights),
        [((tokens, width), F32)] + [((tokens, width), BF)] * 7,
        [pltpu.VMEM((2, tokens, units), BF), pltpu.VMEM((8, tokens, width), F32)],
        4 * tokens * feats * units,
        4 * feats * units,
    )
    return res[0], res[1:]


def add_up(own, received):
    total = own
    for r in received:
        total = total + r.astype(F32)
    return total


def hidden_of(gate, upper, mask):
    sigma = jax.nn.sigmoid(gate)
    return (gate * sigma * upper * mask).astype(BF)


def grads_of(dhid, gate, upper, mask):
    sigma = jax.nn.sigmoid(gate)
    dgate = (dhid * upper * sigma * (1.0 + gate * (1.0 - sigma)) * mask).astype(BF)
    dup = (dhid * gate * sigma * mask).astype(BF)
    return jnp.stack([dgate, dup])


def after(value, *earlier):
    return lax.optimization_barrier((value, earlier))[0]


CORES = [(0, 1), (1, 0), (2, 3), (3, 2)]


def own_half(w, axis, tensor, flip):
    size = w.shape[axis] // 2
    return lax.dynamic_slice_in_dim(w, ((tensor & 1) ^ flip) * size, size, axis)


def hand_out(piece, flip_x, flip_half):
    perm = [
        (
            d * 8 + t,
            ((((t >> 1) & 1) ^ flip_x) * 2 + (t >> 2)) * 8 + 2 * d + ((t & 1) ^ flip_half),
        )
        for d in range(4)
        for t in range(8)
    ]
    return lax.ppermute(piece, ("dp", "tensor"), perm)


def to_sibling(pieces):
    return [lax.ppermute(p, "dp", CORES) for p in pieces]


def body(
    inputs,
    gate_wide,
    up_wide,
    down_wide,
    width_wide,
    gate_narrow,
    up_narrow,
    down_narrow,
    width_narrow,
    cotangent,
):
    section = lax.axis_index("section").astype(jnp.int32)
    tensor = lax.axis_index("tensor").astype(jnp.int32)
    dp = lax.axis_index("dp").astype(jnp.int32)
    mix = (dp & 1) * 4 + (dp >> 1) * 2 + (tensor & 1)
    idx = jnp.stack([section, tensor, mix])
    units_a = gate_wide.shape[1]
    units_b = gate_narrow.shape[1] // 2
    mask_a = (
        tensor * units_a + jnp.arange(units_a, dtype=jnp.int32) < width_wide[0]
    ).astype(F32)
    mask_b = (
        tensor * units_b + jnp.arange(units_b, dtype=jnp.int32) < width_narrow[0]
    ).astype(F32)
    blocks, quarter, width = inputs.shape
    tokens = blocks * quarter
    own_in = inputs.reshape(tokens, width)

    gu_half = [
        jnp.stack([own_half(gate_narrow, 1, tensor, j), own_half(up_narrow, 1, tensor, j)])
        for j in range(2)
    ]
    down_half = [own_half(down_narrow, 0, tensor, j) for j in range(2)]

    gate_wide, up_wide, down_wide = into_vmem(gate_wide, up_wide, down_wide)
    x_chunks = spread(own_in, "tensor", 8)
    first = [hand_out(after(gu_half[j], x_chunks), 0, j) for j in range(2)]
    second = [hand_out(after(gu_half[j], first), 1, j) for j in range(2)]
    gu_b = first + second
    gu_b = gu_b + to_sibling(gu_b)

    own, parts, _ = gate_up(idx, x_chunks, (gate_wide, up_wide), False)
    both_a = add_up(own, after(send(parts, "section", 4), first))
    hidden_a = hidden_of(both_a[0], both_a[1], mask_a)
    own, parts = down_wide_part(idx, spread(hidden_a, "section", 4), down_wide)
    parts = after(parts, second)
    middle = (own_in.astype(F32) + add_up(own, send(parts, "tensor", 8))).astype(BF)

    mid_chunks = spread(middle, "tensor", 8)
    first = [hand_out(after(down_half[j], mid_chunks), 0, j) for j in range(2)]
    second = [hand_out(after(down_half[j], first), 1, j) for j in range(2)]
    down_b = first + second
    down_b = down_b + to_sibling(down_b)
    own, parts, mid_rows = gate_up(idx, mid_chunks, gu_b, True)
    both_b = add_up(own, send(parts, "section", 4))

    cot_chunks = spread(after(cotangent[0], mid_chunks), "tensor", 8)
    own, parts, cot_own = hidden_grad_narrow(idx, cot_chunks, down_b)
    dhid_b = add_up(own, send(parts, "section", 4))

    pair_b = grads_of(dhid_b, both_b[0], both_b[1], mask_b)
    own, parts = input_back_narrow(idx, spread(pair_b, "section", 4), gu_b)
    middle_grad = (cot_own.astype(F32) + add_up(own, send(parts, "tensor", 8))).astype(BF)
    grad_chunks = spread(middle_grad, "tensor", 8)

    hidden_b = after(hidden_of(both_b[0], both_b[1], mask_b), grad_chunks)
    own, parts = down_narrow_part(idx, spread(hidden_b, "section", 4), down_b)
    outputs = (mid_rows.astype(F32) + add_up(own, send(parts, "tensor", 8))).astype(BF)

    own, parts = hidden_grad_wide(idx, grad_chunks, down_wide)
    dhid_a = add_up(own, send(parts, "section", 4))
    pair_a = grads_of(dhid_a, both_a[0], both_a[1], mask_a)
    own, parts = input_back_wide(idx, spread(pair_a, "section", 4), gate_wide, up_wide)
    input_grad = (middle_grad.astype(F32) + add_up(own, send(parts, "tensor", 8))).astype(BF)
    return (
        outputs.reshape(1, quarter, outputs.shape[1]),
        input_grad.reshape(blocks, quarter, width),
    )


def solution(mesh):
    in_specs = (
        P(None, "dp", ("section", "tensor")),
        P("section", "tensor"),
        P("section", "tensor"),
        P("tensor", "section"),
        P(),
        P(("section", "tensor"), "dp"),
        P(("section", "tensor"), "dp"),
        P("dp", ("section", "tensor")),
        P(),
        P("tensor", "dp", "section"),
    )
    out_specs = (P("tensor", "dp", "section"), P(None, "dp", ("section", "tensor")))
    return jax.shard_map(body, mesh=mesh, in_specs=in_specs, out_specs=out_specs, check_vma=False)
```

time: 443 us -> 499 us (1.13)
  waiting for transfers between devices: 130 us -> 175 us
  starting transfers between devices: 226 us -> 242 us
  local copies, waits for them, and re-layouts: 17.1 us -> 30.7 us
  between operations: 16 us -> 3.11 us
  Pallas kernels: 43.1 us -> 31 us
    ppermute x6 -> x16, starting transfers between devices: 6.23 us -> 56.6 us  [the longest x8 45.8 us: hand_out(): return lax.ppermute(piece, ('dp', 'tensor'), perm)]
    ppermute x80, waiting for transfers between devices: 108 us -> 158 us  [send(): lax.ppermute(p, axis, ring(n, r))]
    ppermute x80, starting transfers between devices: 219 us -> 186 us  [send(): lax.ppermute(p, axis, ring(n, r))]
    unnamed x38 -> x112, local copies, waits for them, and re-layouts: 15.6 us -> 29.3 us
    pallas_call x8 -> x9, Pallas kernels: 43.1 us -> 31 us  [the longest x8 29.5 us: call(): pl.pallas_call(kernel, in_specs=[SM] + [VM] * len(operands), out_specs=[V...]
    ppermute x6 -> x16, waiting for transfers between devices: 22.1 us -> 16.4 us  [the longest x8 16.4 us: hand_out(): return lax.ppermute(piece, ('dp', 'tensor'), perm)]
  transfers between devices with their start and end apart: 88 -> 96, of which waited for: 38 -> 47; matrix products, arithmetic and copies ran while one was open for 1% -> 2% of each run, Pallas kernels for 8% -> 5%
where the time goes in v2:
time: 499 us; the launch traced here: 491 us
  starting transfers between devices  242 us (48%)
  waiting for transfers between devices  175 us (35%)
  Pallas kernels  31 us (6%)
  local copies, waits for them, and re-layouts  30.7 us (6%)
  other arithmetic  9.15 us (2%)
    ppermute x80, starting transfers between devices, send(): lax.ppermute(p, axis, ring(n, r))  186 us
    ppermute x80, waiting for transfers between devices, send(): lax.ppermute(p, axis, ring(n, r))  158 us
    ppermute x8, starting transfers between devices, hand_out(): return lax.ppermute(piece, ('dp', 'tensor'), perm)  45.8 us
    pallas_call x8, Pallas kernels, call(): pl.pallas_call(kernel, in_specs=[SM] + [VM] * len(operands), out_specs=[V...  29.5 us
    unnamed x112, local copies, waits for them, and re-layouts  29.3 us
    ppermute x8, waiting for transfers between devices, hand_out(): return lax.ppermute(piece, ('dp', 'tensor'), perm)  16.4 us
    ppermute x8, starting transfers between devices, to_sibling(): return [lax.ppermute(p, 'dp', CORES) for p in pieces]  10.8 us
  transfers between devices with their start and end apart: 96, of which 47 were waited for; matrix products, arithmetic and copies ran while one was open for 2% of the time, Pallas kernels for 5%

profile of v2, /device:TPU:0, one launch (start us, length us, event | category | flops | bytes accessed | tf_op | source)
XLA Modules:
  0.0 490.9 jit_solution(1953562728164237235)
XLA Ops:
  2.4 2.9 collective-permute-start.1
  9.7 3.1 copy-done.4
  12.8 3.1 copy-done.5
  15.8 3.1 copy-done.6
  32.4 6.1 %shard_map.114 = (f32[2,64,1792]{2,1,0:T(8,128)S(1)}, bf16[2,64,1792]{2,1,0:T(8,128)(2,1)}, bf16[2,64,1792]{2,1,0:T(8,128)(2,1)}, bf16[2,64,1792]{2,1,0:T(8,128)(2,1)S(1)}, bf16[32,2048]{1,0:T(8,128)(2,1)}) custom-call(s32[3]{0:T(128)S(1)} %pad_add_fusion.idx_ref, bf16[256,256]{1,0:T(8,128)(2,1)S(1)} %bitcast.82, ...), custom_call_target="tpu_custom_call" | custom-call | flops 3758096384 | bytes 14680064 | tf_op jit(solution)/shard_map/pallas_call | solution.py:58
  41.5 3.6 collective-permute-start.8
  46.7 4.0 collective-permute-done.7
  50.7 11.6 %collective-permute-done.8 = bf16[2,64,1792]{2,1,0:T(8,128)(2,1)S(1)} collective-permute-done((bf16[2,64,1792]{2,1,0:T(8,128)(2,1)}, bf16[2,64,1792]{2,1,0:T(8,128)(2,1)S(1)}, u32[]{:S(2)}, u32[]{:S(2)}) %collective-permute-start.8) | collective-permute-done | bytes 458784 | tf_op jit(solution)/shard_map/ppermute | solution.py:19
  64.8 9.0 %collective-permute-done.11.refs_9_.refs_5_ = bf16[2,256,896]{2,1,0:T(8,128)(2,1)S(1)} collective-permute-done((bf16[2,256,896]{2,1,0:T(8,128)(2,1)}, bf16[2,256,896]{2,1,0:T(8,128)(2,1)S(1)}, u32[]{:S(2)}, u32[]{:S(2)}) %collective-permute-start.11) | collective-permute-done | bytes 917536 | tf_op jit(solution)/shard_map/ppermute | solution.py:373
  73.8 39.3 %collective-permute-start.15 = (bf16[2,256,896]{2,1,0:T(8,128)(2,1)}, bf16[2,256,896]{2,1,0:T(8,128)(2,1)S(1)}, u32[]{:S(2)}, u32[]{:S(2)}) collective-permute-start(bf16[2,256,896]{2,1,0:T(8,128)(2,1)} %pad_maximum_fusion), channel_id=1, source_target_pairs={{0,16},{1,17},{2,0},{3,1},{4,24},{5,25},{6,8},{7,9},{8,18},{9,19},... | collective-permute-start | bytes 2752520 | tf_op jit(solution)/shard_map/ppermute | solution.py:373
  118.5 3.6 collective-permute-start.13
  124.6 5.7 %collective-permute-done.13.refs_2_ = bf16[64,1792]{1,0:T(8,128)(2,1)S(1)} collective-permute-done((bf16[64,1792]{1,0:T(8,128)(2,1)S(1)}, bf16[64,1792]{1,0:T(8,128)(2,1)S(1)}, u32[]{:S(2)}, u32[]{:S(2)}) %collective-permute-start.13) | collective-permute-done | bytes 229408 | tf_op jit(solution)/shard_map/ppermute | solution.py:19
  130.9 3.1 copy-done.3
  136.7 7.4 %collective-permute-done.16.refs_11_.refs_7_ = bf16[2,256,896]{2,1,0:T(8,128)(2,1)S(1)} collective-permute-done((bf16[2,256,896]{2,1,0:T(8,128)(2,1)}, bf16[2,256,896]{2,1,0:T(8,128)(2,1)S(1)}, u32[]{:S(2)}, u32[]{:S(2)}) %collective-permute-start.16) | collective-permute-done | bytes 917536 | tf_op jit(solution)/shard_map/ppermute | solution.py:373
  144.0 38.6 %collective-permute-start.23 = (bf16[256,256]{1,0:T(8,128)(2,1)S(1)}, bf16[256,256]{1,0:T(8,128)(2,1)S(1)}, u32[]{:S(2)}, u32[]{:S(2)}) collective-permute-start(bf16[256,256]{1,0:T(8,128)(2,1)S(1)} %get-tuple-element.103), channel_id=1, source_target_pairs={{0,7},{1,0},{2,1},{3,2},{4,3},{5,4},{6,5},{7,6},{8,15},{9,8},{10,9... | collective-permute-start | bytes 393224 | tf_op jit(solution)/shard_map/ppermute | solution.py:19
  195.1 4.3 collective-permute-done.18
  204.0 4.4 collective-permute-done.24.refs_1_
  222.3 9.7 %collective-permute-start.34 = (bf16[2,256,896]{2,1,0:T(8,128)(2,1)S(1)}, bf16[2,256,896]{2,1,0:T(8,128)(2,1)S(1)}, u32[]{:S(2)}, u32[]{:S(2)}) collective-permute-start(bf16[2,256,896]{2,1,0:T(8,128)(2,1)S(1)} %collective-permute-done.16.refs_11_.refs_7_), channel_id=1, source_target_pairs={{0,8},{8,0},{16,24},{24,16},{1,9},{9,1},{17,25},{25,17},{2,10},{10... | collective-permute-start | bytes 2752520 | tf_op jit(solution)/shard_map/ppermute | solution.py:377
  233.0 12.4 %collective-permute-done.38.refs_1_ = bf16[32,2048]{1,0:T(8,128)(2,1)S(1)} collective-permute-done((bf16[32,2048]{1,0:T(8,128)(2,1)S(1)}, bf16[32,2048]{1,0:T(8,128)(2,1)S(1)}, u32[]{:S(2)}, u32[]{:S(2)}) %collective-permute-start.38) | collective-permute-done | bytes 131104 | tf_op jit(solution)/shard_map/ppermute | solution.py:19
  248.0 6.6 %collective-permute-start.40 = (bf16[32,2048]{1,0:T(8,128)(2,1)S(1)}, bf16[32,2048]{1,0:T(8,128)(2,1)S(1)}, u32[]{:S(2)}, u32[]{:S(2)}) collective-permute-start(bf16[32,2048]{1,0:T(8,128)(2,1)S(1)} %bitcast.85), channel_id=1, source_target_pairs={{0,3},{1,4},{2,5},{3,6},{4,7},{5,0},{6,1},{7,2},{8,11},{9,12},{10,... | collective-permute-start | bytes 393224 | tf_op jit(solution)/shard_map/ppermute | solution.py:19
  254.7 14.8 %collective-permute-start.41 = (bf16[32,2048]{1,0:T(8,128)(2,1)S(1)}, bf16[32,2048]{1,0:T(8,128)(2,1)S(1)}, u32[]{:S(2)}, u32[]{:S(2)}) collective-permute-start(bf16[32,2048]{1,0:T(8,128)(2,1)S(1)} %bitcast.86), channel_id=1, source_target_pairs={{0,4},{1,5},{2,6},{3,7},{4,0},{5,1},{6,2},{7,3},{8,12},{9,13},{10,... | collective-permute-start | bytes 393224 | tf_op jit(solution)/shard_map/ppermute | solution.py:19
  275.5 22.1 %collective-permute-done.42.refs_5_ = bf16[32,2048]{1,0:T(8,128)(2,1)S(1)} collective-permute-done((bf16[32,2048]{1,0:T(8,128)(2,1)S(1)}, bf16[32,2048]{1,0:T(8,128)(2,1)S(1)}, u32[]{:S(2)}, u32[]{:S(2)}) %collective-permute-start.42) | collective-permute-done | bytes 131104 | tf_op jit(solution)/shard_map/ppermute | solution.py:19
  298.3 6.5 %collective-permute-done.43.refs_6_ = bf16[32,2048]{1,0:T(8,128)(2,1)S(1)} collective-permute-done((bf16[32,2048]{1,0:T(8,128)(2,1)S(1)}, bf16[32,2048]{1,0:T(8,128)(2,1)S(1)}, u32[]{:S(2)}, u32[]{:S(2)}) %collective-permute-start.43) | collective-permute-done | bytes 131104 | tf_op jit(solution)/shard_map/ppermute | solution.py:19
  306.6 5.2 %collective-permute-start.44 = (bf16[32,2048]{1,0:T(8,128)(2,1)S(1)}, bf16[32,2048]{1,0:T(8,128)(2,1)S(1)}, u32[]{:S(2)}, u32[]{:S(2)}) collective-permute-start(bf16[32,2048]{1,0:T(8,128)(2,1)S(1)} %bitcast.89), channel_id=1, source_target_pairs={{0,7},{1,0},{2,1},{3,2},{4,3},{5,4},{6,5},{7,6},{8,15},{9,8},{10,9... | collective-permute-start | bytes 393224 | tf_op jit(solution)/shard_map/ppermute | solution.py:19
  311.8 4.1 shard_map.116
  318.0 4.0 collective-permute-start.37
  334.7 3.0 shard_map.117
  352.8 8.4 %collective-permute-done.56.refs_1_ = bf16[2,64,896]{2,1,0:T(8,128)(2,1)S(1)} collective-permute-done((bf16[2,64,896]{2,1,0:T(8,128)(2,1)S(1)}, bf16[2,64,896]{2,1,0:T(8,128)(2,1)S(1)}, u32[]{:S(2)}, u32[]{:S(2)}) %collective-permute-start.56) | collective-permute-done | bytes 229408 | tf_op jit(solution)/shard_map/ppermute | solution.py:19
  361.9 3.1 shard_map.118
  377.9 5.6 %collective-permute-done.60 = bf16[256,256]{1,0:T(8,128)(2,1)S(1)} collective-permute-done((bf16[256,256]{1,0:T(8,128)(2,1)S(1)}, bf16[256,256]{1,0:T(8,128)(2,1)S(1)}, u32[]{:S(2)}, u32[]{:S(2)}) %collective-permute-start.60) | collective-permute-done | bytes 131104 | tf_op jit(solution)/shard_map/ppermute | solution.py:19
  384.0 3.0 collective-permute-start.68
  389.2 3.3 collective-permute-done.66.refs_1_
  392.9 5.5 %collective-permute-start.72 = (bf16[256,256]{1,0:T(8,128)(2,1)S(1)}, bf16[256,256]{1,0:T(8,128)(2,1)S(1)}, u32[]{:S(2)}, u32[]{:S(2)}) collective-permute-start(bf16[256,256]{1,0:T(8,128)(2,1)S(1)} %add_convert_fusion.2.refs_0_), channel_id=1, source_target_pairs={{0,7},{1,0},{2,1},{3,2},{4,3},{5,4},{6,5},{7,6},{8,15},{9,8},{10,9... | collective-permute-start | bytes 393224 | tf_op jit(solution)/shard_map/ppermute | solution.py:19
  401.0 3.0 shard_map.120
  403.9 2.8 collective-permute-start.85
  407.7 5.1 %collective-permute-done.85 = bf16[64,1792]{1,0:T(8,128)(2,1)S(1)} collective-permute-done((bf16[64,1792]{1,0:T(8,128)(2,1)S(1)}, bf16[64,1792]{1,0:T(8,128)(2,1)S(1)}, u32[]{:S(2)}, u32[]{:S(2)}) %collective-permute-start.85) | collective-permute-done | bytes 229408 | tf_op jit(solution)/shard_map/ppermute | solution.py:19
  415.2 3.3 collective-permute-done.83
  419.0 3.6 collective-permute-start.87
  425.2 14.9 %collective-permute-done.73.refs_1_ = bf16[64,896]{1,0:T(8,128)(2,1)S(1)} collective-permute-done((bf16[64,896]{1,0:T(8,128)(2,1)S(1)}, bf16[64,896]{1,0:T(8,128)(2,1)S(1)}, u32[]{:S(2)}, u32[]{:S(2)}) %collective-permute-start.73) | collective-permute-done | bytes 114720 | tf_op jit(solution)/shard_map/ppermute | solution.py:19
  441.4 3.5 collective-permute-done.75.refs_3_
  444.9 2.8 shard_map.119
  447.7 4.6 collective-permute-start.82
  452.3 3.8 collective-permute-start.81
  456.2 2.9 collective-permute-start.80
  461.9 4.6 shard_map.121
  467.6 3.6 collective-permute-start.95
  475.5 2.9 collective-permute-done.76
  478.4 4.2 collective-permute-start.90
  (286 shorter events, 152.1 us)
Async XLA Ops:
  0.6 21.4 %collective-permute-start = (bf16[256,256]{1,0:T(8,128)(2,1)}, bf16[256,256]{1,0:T(8,128)(2,1)S(1)}, u32[]{:S(2)}, u32[]{:S(2)}) collective-permute-start(bf16[256,256]{1,0:T(8,128)(2,1)} %bitcast.75), channel_id=1, source_target_pairs={{0,1},{1,2},{2,3},{3,4},{4,5},{5,6},{6,7},{7,0},{8,9},{9,10},{10,1... | collective-permute-start | bytes 393224 | tf_op jit(solution)/shard_map/ppermute | solution.py:19
  2.4 21.3 %collective-permute-start.1 = (bf16[256,256]{1,0:T(8,128)(2,1)}, bf16[256,256]{1,0:T(8,128)(2,1)S(1)}, u32[]{:S(2)}, u32[]{:S(2)}) collective-permute-start(bf16[256,256]{1,0:T(8,128)(2,1)} %bitcast.76), channel_id=1, source_target_pairs={{0,2},{1,3},{2,4},{3,5},{4,6},{5,7},{6,0},{7,1},{8,10},{9,11},{10,... | collective-permute-start | bytes 393224 | tf_op jit(solution)/shard_map/ppermute | solution.py:19
  5.3 21.8 %collective-permute-start.2 = (bf16[256,256]{1,0:T(8,128)(2,1)}, bf16[256,256]{1,0:T(8,128)(2,1)S(1)}, u32[]{:S(2)}, u32[]{:S(2)}) collective-permute-start(bf16[256,256]{1,0:T(8,128)(2,1)} %bitcast.77), channel_id=1, source_target_pairs={{0,3},{1,4},{2,5},{3,6},{4,7},{5,0},{6,1},{7,2},{8,11},{9,12},{10,... | collective-permute-start | bytes 393224 | tf_op jit(solution)/shard_map/ppermute | solution.py:19
  7.5 19.6 %collective-permute-start.3 = (bf16[256,256]{1,0:T(8,128)(2,1)}, bf16[256,256]{1,0:T(8,128)(2,1)S(1)}, u32[]{:S(2)}, u32[]{:S(2)}) collective-permute-start(bf16[256,256]{1,0:T(8,128)(2,1)} %bitcast.78), channel_id=1, source_target_pairs={{0,4},{1,5},{2,6},{3,7},{4,0},{5,1},{6,2},{7,3},{8,12},{9,13},{10,... | collective-permute-start | bytes 393224 | tf_op jit(solution)/shard_map/ppermute | solution.py:19
  8.1 19.0 %collective-permute-start.4 = (bf16[256,256]{1,0:T(8,128)(2,1)}, bf16[256,256]{1,0:T(8,128)(2,1)S(1)}, u32[]{:S(2)}, u32[]{:S(2)}) collective-permute-start(bf16[256,256]{1,0:T(8,128)(2,1)} %bitcast.79), channel_id=1, source_target_pairs={{0,5},{1,6},{2,7},{3,0},{4,1},{5,2},{6,3},{7,4},{8,13},{9,14},{10,... | collective-permute-start | bytes 393224 | tf_op jit(solution)/shard_map/ppermute | solution.py:19
  30.1 34.7 %collective-permute-start.10 = (bf16[2,256,896]{2,1,0:T(8,128)(2,1)}, bf16[2,256,896]{2,1,0:T(8,128)(2,1)S(1)}, u32[]{:S(2)}, u32[]{:S(2)}) collective-permute-start(bf16[2,256,896]{2,1,0:T(8,128)(2,1)} %pad_maximum_fusion), channel_id=1, source_target_pairs={{0,0},{1,1},{2,16},{3,17},{4,8},{5,9},{6,24},{7,25},{8,2},{9,3},{1... | collective-permute-start | bytes 2752520 | tf_op jit(solution)/shard_map/ppermute | solution.py:373
  31.9 41.9 %collective-permute-start.11 = (bf16[2,256,896]{2,1,0:T(8,128)(2,1)}, bf16[2,256,896]{2,1,0:T(8,128)(2,1)S(1)}, u32[]{:S(2)}, u32[]{:S(2)}) collective-permute-start(bf16[2,256,896]{2,1,0:T(8,128)(2,1)} %pad_maximum_fusion.1), channel_id=1, source_target_pairs={{0,1},{1,0},{2,17},{3,16},{4,9},{5,8},{6,25},{7,24},{8,3},{9,2},{1... | collective-permute-start | bytes 2752520 | tf_op jit(solution)/shard_map/ppermute | solution.py:373
  41.5 20.8 %collective-permute-start.8 = (bf16[2,64,1792]{2,1,0:T(8,128)(2,1)}, bf16[2,64,1792]{2,1,0:T(8,128)(2,1)S(1)}, u32[]{:S(2)}, u32[]{:S(2)}) collective-permute-start(bf16[2,64,1792]{2,1,0:T(8,128)(2,1)} %get-tuple-element.79), channel_id=1, source_target_pairs={{0,64},{32,96},{64,0},{96,32},{1,65},{33,97},{65,1},{97,33},{2,66}... | collective-permute-start | bytes 1376264 | tf_op jit(solution)/shard_map/ppermute | solution.py:19
  45.1 19.7 %collective-permute-start.9 = (bf16[2,64,1792]{2,1,0:T(8,128)(2,1)S(1)}, bf16[2,64,1792]{2,1,0:T(8,128)(2,1)}, u32[]{:S(2)}, u32[]{:S(2)}) collective-permute-start(bf16[2,64,1792]{2,1,0:T(8,128)(2,1)S(1)} %get-tuple-element.80), channel_id=1, source_target_pairs={{0,96},{32,0},{64,32},{96,64},{1,97},{33,1},{65,33},{97,65},{2,98}... | collective-permute-start | bytes 1376264 | tf_op jit(solution)/shard_map/ppermute | solution.py:19
  73.8 62.9 %collective-permute-start.15 = (bf16[2,256,896]{2,1,0:T(8,128)(2,1)}, bf16[2,256,896]{2,1,0:T(8,128)(2,1)S(1)}, u32[]{:S(2)}, u32[]{:S(2)}) collective-permute-start(bf16[2,256,896]{2,1,0:T(8,128)(2,1)} %pad_maximum_fusion), channel_id=1, source_target_pairs={{0,16},{1,17},{2,0},{3,1},{4,24},{5,25},{6,8},{7,9},{8,18},{9,19},... | collective-permute-start | bytes 2752520 | tf_op jit(solution)/shard_map/ppermute | solution.py:373
  113.1 30.9 %collective-permute-start.16 = (bf16[2,256,896]{2,1,0:T(8,128)(2,1)}, bf16[2,256,896]{2,1,0:T(8,128)(2,1)S(1)}, u32[]{:S(2)}, u32[]{:S(2)}) collective-permute-start(bf16[2,256,896]{2,1,0:T(8,128)(2,1)} %pad_maximum_fusion.1), channel_id=1, source_target_pairs={{0,17},{1,16},{2,1},{3,0},{4,25},{5,24},{6,9},{7,8},{8,19},{9,18},... | collective-permute-start | bytes 2752520 | tf_op jit(solution)/shard_map/ppermute | solution.py:373
  118.5 11.8 %collective-permute-start.13 = (bf16[64,1792]{1,0:T(8,128)(2,1)S(1)}, bf16[64,1792]{1,0:T(8,128)(2,1)S(1)}, u32[]{:S(2)}, u32[]{:S(2)}) collective-permute-start(bf16[64,1792]{1,0:T(8,128)(2,1)S(1)} %multiply_convert_fusion.2.refs_0_), channel_id=1, source_target_pairs={{0,64},{32,96},{64,0},{96,32},{1,65},{33,97},{65,1},{97,33},{2,66}... | collective-permute-start | bytes 688136 | tf_op jit(solution)/shard_map/ppermute | solution.py:19
  144.0 44.7 %collective-permute-start.23 = (bf16[256,256]{1,0:T(8,128)(2,1)S(1)}, bf16[256,256]{1,0:T(8,128)(2,1)S(1)}, u32[]{:S(2)}, u32[]{:S(2)}) collective-permute-start(bf16[256,256]{1,0:T(8,128)(2,1)S(1)} %get-tuple-element.103), channel_id=1, source_target_pairs={{0,7},{1,0},{2,1},{3,2},{4,3},{5,4},{6,5},{7,6},{8,15},{9,8},{10,9... | collective-permute-start | bytes 393224 | tf_op jit(solution)/shard_map/ppermute | solution.py:19
  192.5 29.8 %collective-permute-start.31 = (bf16[2,256,896]{2,1,0:T(8,128)(2,1)S(1)}, bf16[2,256,896]{2,1,0:T(8,128)(2,1)S(1)}, u32[]{:S(2)}, u32[]{:S(2)}) collective-permute-start(bf16[2,256,896]{2,1,0:T(8,128)(2,1)S(1)} %collective-permute-done.10.refs_8_.refs_4_), channel_id=1, source_target_pairs={{0,8},{8,0},{16,24},{24,16},{1,9},{9,1},{17,25},{25,17},{2,10},{10... | collective-permute-start | bytes 2752520 | tf_op jit(solution)/shard_map/ppermute | solution.py:377
  193.8 38.2 %collective-permute-start.32 = (bf16[2,256,896]{2,1,0:T(8,128)(2,1)S(1)}, bf16[2,256,896]{2,1,0:T(8,128)(2,1)S(1)}, u32[]{:S(2)}, u32[]{:S(2)}) collective-permute-start(bf16[2,256,896]{2,1,0:T(8,128)(2,1)S(1)} %collective-permute-done.11.refs_9_.refs_5_), channel_id=1, source_target_pairs={{0,8},{8,0},{16,24},{24,16},{1,9},{9,1},{17,25},{25,17},{2,10},{10... | collective-permute-start | bytes 2752520 | tf_op jit(solution)/shard_map/ppermute | solution.py:377
  210.6 94.9 %collective-permute-start.33 = (bf16[2,256,896]{2,1,0:T(8,128)(2,1)S(1)}, bf16[2,256,896]{2,1,0:T(8,128)(2,1)S(1)}, u32[]{:S(2)}, u32[]{:S(2)}) collective-permute-start(bf16[2,256,896]{2,1,0:T(8,128)(2,1)S(1)} %collective-permute-done.15.refs_10_.refs_6_), channel_id=1, source_target_pairs={{0,8},{8,0},{16,24},{24,16},{1,9},{9,1},{17,25},{25,17},{2,10},{10... | collective-permute-start | bytes 2752520 | tf_op jit(solution)/shard_map/ppermute | solution.py:377
  221.0 27.0 %collective-permute-start.45 = (bf16[896,256]{1,0:T(8,128)(2,1)S(1)}, bf16[896,256]{1,0:T(8,128)(2,1)S(1)}, u32[]{:S(2)}, u32[]{:S(2)}) collective-permute-start(bf16[896,256]{1,0:T(8,128)(2,1)S(1)} %get-tuple-element.112), channel_id=1, source_target_pairs={{0,0},{1,1},{2,16},{3,17},{4,8},{5,9},{6,24},{7,25},{8,2},{9,3},{1... | collective-permute-start | bytes 1376264 | tf_op jit(solution)/shard_map/ppermute | solution.py:373
  221.7 32.9 %collective-permute-start.46 = (bf16[896,256]{1,0:T(8,128)(2,1)S(1)}, bf16[896,256]{1,0:T(8,128)(2,1)S(1)}, u32[]{:S(2)}, u32[]{:S(2)}) collective-permute-start(bf16[896,256]{1,0:T(8,128)(2,1)S(1)} %get-tuple-element.113), channel_id=1, source_target_pairs={{0,1},{1,0},{2,17},{3,16},{4,9},{5,8},{6,25},{7,24},{8,3},{9,2},{1... | collective-permute-start | bytes 1376264 | tf_op jit(solution)/shard_map/ppermute | solution.py:373
  222.3 84.3 %collective-permute-start.34 = (bf16[2,256,896]{2,1,0:T(8,128)(2,1)S(1)}, bf16[2,256,896]{2,1,0:T(8,128)(2,1)S(1)}, u32[]{:S(2)}, u32[]{:S(2)}) collective-permute-start(bf16[2,256,896]{2,1,0:T(8,128)(2,1)S(1)} %collective-permute-done.16.refs_11_.refs_7_), channel_id=1, source_target_pairs={{0,8},{8,0},{16,24},{24,16},{1,9},{9,1},{17,25},{25,17},{2,10},{10... | collective-permute-start | bytes 2752520 | tf_op jit(solution)/shard_map/ppermute | solution.py:377
  232.0 13.4 %collective-permute-start.38 = (bf16[32,2048]{1,0:T(8,128)(2,1)S(1)}, bf16[32,2048]{1,0:T(8,128)(2,1)S(1)}, u32[]{:S(2)}, u32[]{:S(2)}) collective-permute-start(bf16[32,2048]{1,0:T(8,128)(2,1)S(1)} %bitcast.83), channel_id=1, source_target_pairs={{0,1},{1,2},{2,3},{3,4},{4,5},{5,6},{6,7},{7,0},{8,9},{9,10},{10,1... | collective-permute-start | bytes 393224 | tf_op jit(solution)/shard_map/ppermute | solution.py:19
  245.3 24.1 %collective-permute-start.39 = (bf16[32,2048]{1,0:T(8,128)(2,1)S(1)}, bf16[32,2048]{1,0:T(8,128)(2,1)S(1)}, u32[]{:S(2)}, u32[]{:S(2)}) collective-permute-start(bf16[32,2048]{1,0:T(8,128)(2,1)S(1)} %bitcast.84), channel_id=1, source_target_pairs={{0,2},{1,3},{2,4},{3,5},{4,6},{5,7},{6,0},{7,1},{8,10},{9,11},{10,... | collective-permute-start | bytes 393224 | tf_op jit(solution)/shard_map/ppermute | solution.py:19
  248.0 22.1 %collective-permute-start.40 = (bf16[32,2048]{1,0:T(8,128)(2,1)S(1)}, bf16[32,2048]{1,0:T(8,128)(2,1)S(1)}, u32[]{:S(2)}, u32[]{:S(2)}) collective-permute-start(bf16[32,2048]{1,0:T(8,128)(2,1)S(1)} %bitcast.85), channel_id=1, source_target_pairs={{0,3},{1,4},{2,5},{3,6},{4,7},{5,0},{6,1},{7,2},{8,11},{9,12},{10,... | collective-permute-start | bytes 393224 | tf_op jit(solution)/shard_map/ppermute | solution.py:19
  254.7 17.7 %collective-permute-start.41 = (bf16[32,2048]{1,0:T(8,128)(2,1)S(1)}, bf16[32,2048]{1,0:T(8,128)(2,1)S(1)}, u32[]{:S(2)}, u32[]{:S(2)}) collective-permute-start(bf16[32,2048]{1,0:T(8,128)(2,1)S(1)} %bitcast.86), channel_id=1, source_target_pairs={{0,4},{1,5},{2,6},{3,7},{4,0},{5,1},{6,2},{7,3},{8,12},{9,13},{10,... | collective-permute-start | bytes 393224 | tf_op jit(solution)/shard_map/ppermute | solution.py:19
  270.1 35.9 %collective-permute-start.47 = (bf16[896,256]{1,0:T(8,128)(2,1)S(1)}, bf16[896,256]{1,0:T(8,128)(2,1)}, u32[]{:S(2)}, u32[]{:S(2)}) collective-permute-start(bf16[896,256]{1,0:T(8,128)(2,1)S(1)} %get-tuple-element.112), channel_id=1, source_target_pairs={{0,16},{1,17},{2,0},{3,1},{4,24},{5,25},{6,8},{7,9},{8,18},{9,19},... | collective-permute-start | bytes 1376264 | tf_op jit(solution)/shard_map/ppermute | solution.py:373
  270.8 35.4 %collective-permute-start.48 = (bf16[896,256]{1,0:T(8,128)(2,1)S(1)}, bf16[896,256]{1,0:T(8,128)(2,1)}, u32[]{:S(2)}, u32[]{:S(2)}) collective-permute-start(bf16[896,256]{1,0:T(8,128)(2,1)S(1)} %get-tuple-element.113), channel_id=1, source_target_pairs={{0,17},{1,16},{2,1},{3,0},{4,25},{5,24},{6,9},{7,8},{8,19},{9,18},... | collective-permute-start | bytes 1376264 | tf_op jit(solution)/shard_map/ppermute | solution.py:373
  273.1 24.6 %collective-permute-start.42 = (bf16[32,2048]{1,0:T(8,128)(2,1)S(1)}, bf16[32,2048]{1,0:T(8,128)(2,1)S(1)}, u32[]{:S(2)}, u32[]{:S(2)}) collective-permute-start(bf16[32,2048]{1,0:T(8,128)(2,1)S(1)} %bitcast.87), channel_id=1, source_target_pairs={{0,5},{1,6},{2,7},{3,0},{4,1},{5,2},{6,3},{7,4},{8,13},{9,14},{10,... | collective-permute-start | bytes 393224 | tf_op jit(solution)/shard_map/ppermute | solution.py:19
  305.4 16.7 %collective-permute-start.49 = (bf16[896,256]{1,0:T(8,128)(2,1)S(1)}, bf16[896,256]{1,0:T(8,128)(2,1)S(1)}, u32[]{:S(2)}, u32[]{:S(2)}) collective-permute-start(bf16[896,256]{1,0:T(8,128)(2,1)S(1)} %collective-permute-done.45.refs_8_.refs_4_), channel_id=1, source_target_pairs={{0,8},{8,0},{16,24},{24,16},{1,9},{9,1},{17,25},{25,17},{2,10},{10... | collective-permute-start | bytes 1376264 | tf_op jit(solution)/shard_map/ppermute | solution.py:377
  305.6 17.3 %collective-permute-start.50 = (bf16[896,256]{1,0:T(8,128)(2,1)S(1)}, bf16[896,256]{1,0:T(8,128)(2,1)S(1)}, u32[]{:S(2)}, u32[]{:S(2)}) collective-permute-start(bf16[896,256]{1,0:T(8,128)(2,1)S(1)} %collective-permute-done.46.refs_9_.refs_5_), channel_id=1, source_target_pairs={{0,8},{8,0},{16,24},{24,16},{1,9},{9,1},{17,25},{25,17},{2,10},{10... | collective-permute-start | bytes 1376264 | tf_op jit(solution)/shard_map/ppermute | solution.py:377
  306.1 19.7 %collective-permute-start.51 = (bf16[896,256]{1,0:T(8,128)(2,1)}, bf16[896,256]{1,0:T(8,128)(2,1)}, u32[]{:S(2)}, u32[]{:S(2)}) collective-permute-start(bf16[896,256]{1,0:T(8,128)(2,1)} %collective-permute-done.47.refs_10_.refs_6_), channel_id=1, source_target_pairs={{0,8},{8,0},{16,24},{24,16},{1,9},{9,1},{17,25},{25,17},{2,10},{10... | collective-permute-start | bytes 1376264 | tf_op jit(solution)/shard_map/ppermute | solution.py:377
  306.2 19.6 %collective-permute-start.52 = (bf16[896,256]{1,0:T(8,128)(2,1)}, bf16[896,256]{1,0:T(8,128)(2,1)}, u32[]{:S(2)}, u32[]{:S(2)}) collective-permute-start(bf16[896,256]{1,0:T(8,128)(2,1)} %collective-permute-done.48.refs_11_.refs_7_), channel_id=1, source_target_pairs={{0,8},{8,0},{16,24},{24,16},{1,9},{9,1},{17,25},{25,17},{2,10},{10... | collective-permute-start | bytes 1376264 | tf_op jit(solution)/shard_map/ppermute | solution.py:377
  318.0 24.0 %collective-permute-start.37 = (bf16[2,64,896]{2,1,0:T(8,128)(2,1)}, bf16[2,64,896]{2,1,0:T(8,128)(2,1)}, u32[]{:S(2)}, u32[]{:S(2)}) collective-permute-start(bf16[2,64,896]{2,1,0:T(8,128)(2,1)} %get-tuple-element.108), channel_id=1, source_target_pairs={{0,96},{32,0},{64,32},{96,64},{1,97},{33,1},{65,33},{97,65},{2,98}... | collective-permute-start | bytes 688136 | tf_op jit(solution)/shard_map/ppermute | solution.py:19
  322.8 19.2 %collective-permute-start.36 = (bf16[2,64,896]{2,1,0:T(8,128)(2,1)}, bf16[2,64,896]{2,1,0:T(8,128)(2,1)}, u32[]{:S(2)}, u32[]{:S(2)}) collective-permute-start(bf16[2,64,896]{2,1,0:T(8,128)(2,1)} %get-tuple-element.107), channel_id=1, source_target_pairs={{0,64},{32,96},{64,0},{96,32},{1,65},{33,97},{65,1},{97,33},{2,66}... | collective-permute-start | bytes 688136 | tf_op jit(solution)/shard_map/ppermute | solution.py:19
  323.6 18.4 %collective-permute-start.35 = (bf16[2,64,896]{2,1,0:T(8,128)(2,1)}, bf16[2,64,896]{2,1,0:T(8,128)(2,1)}, u32[]{:S(2)}, u32[]{:S(2)}) collective-permute-start(bf16[2,64,896]{2,1,0:T(8,128)(2,1)} %get-tuple-element.106), channel_id=1, source_target_pairs={{0,32},{32,64},{64,96},{96,0},{1,33},{33,65},{65,97},{97,1},{2,34}... | collective-permute-start | bytes 688136 | tf_op jit(solution)/shard_map/ppermute | solution.py:19
  348.6 12.7 %collective-permute-start.56 = (bf16[2,64,896]{2,1,0:T(8,128)(2,1)S(1)}, bf16[2,64,896]{2,1,0:T(8,128)(2,1)S(1)}, u32[]{:S(2)}, u32[]{:S(2)}) collective-permute-start(bf16[2,64,896]{2,1,0:T(8,128)(2,1)S(1)} %pad_maximum_fusion.3.refs_0_), channel_id=1, source_target_pairs={{0,32},{32,64},{64,96},{96,0},{1,33},{33,65},{65,97},{97,1},{2,34}... | collective-permute-start | bytes 688136 | tf_op jit(solution)/shard_map/ppermute | solution.py:19
  349.0 12.3 %collective-permute-start.57 = (bf16[2,64,896]{2,1,0:T(8,128)(2,1)S(1)}, bf16[2,64,896]{2,1,0:T(8,128)(2,1)S(1)}, u32[]{:S(2)}, u32[]{:S(2)}) collective-permute-start(bf16[2,64,896]{2,1,0:T(8,128)(2,1)S(1)} %pad_maximum_fusion.3.refs_0_), channel_id=1, source_target_pairs={{0,64},{32,96},{64,0},{96,32},{1,65},{33,97},{65,1},{97,33},{2,66}... | collective-permute-start | bytes 688136 | tf_op jit(solution)/shard_map/ppermute | solution.py:19
  370.7 12.9 %collective-permute-start.60 = (bf16[256,256]{1,0:T(8,128)(2,1)S(1)}, bf16[256,256]{1,0:T(8,128)(2,1)S(1)}, u32[]{:S(2)}, u32[]{:S(2)}) collective-permute-start(bf16[256,256]{1,0:T(8,128)(2,1)S(1)} %get-tuple-element.121), channel_id=1, source_target_pairs={{0,2},{1,3},{2,4},{3,5},{4,6},{5,7},{6,0},{7,1},{8,10},{9,11},{10,... | collective-permute-start | bytes 393224 | tf_op jit(solution)/shard_map/ppermute | solution.py:19
  384.0 14.4 %collective-permute-start.68 = (bf16[256,256]{1,0:T(8,128)(2,1)S(1)}, bf16[256,256]{1,0:T(8,128)(2,1)S(1)}, u32[]{:S(2)}, u32[]{:S(2)}) collective-permute-start(bf16[256,256]{1,0:T(8,128)(2,1)S(1)} %add_convert_fusion.2.refs_0_), channel_id=1, source_target_pairs={{0,3},{1,4},{2,5},{3,6},{4,7},{5,0},{6,1},{7,2},{8,11},{9,12},{10,... | collective-permute-start | bytes 393224 | tf_op jit(solution)/shard_map/ppermute | solution.py:19
  418.9 37.3 %collective-permute-start.86 = (bf16[2,64,1792]{2,1,0:T(8,128)(2,1)S(1)}, bf16[2,64,1792]{2,1,0:T(8,128)(2,1)S(1)}, u32[]{:S(2)}, u32[]{:S(2)}) collective-permute-start(bf16[2,64,1792]{2,1,0:T(8,128)(2,1)S(1)} %pad_maximum_fusion.2.refs_0_), channel_id=1, source_target_pairs={{0,32},{32,64},{64,96},{96,0},{1,33},{33,65},{65,97},{97,1},{2,34}... | collective-permute-start | bytes 1376264 | tf_op jit(solution)/shard_map/ppermute | solution.py:19
  419.0 40.1 %collective-permute-start.87 = (bf16[2,64,1792]{2,1,0:T(8,128)(2,1)S(1)}, bf16[2,64,1792]{2,1,0:T(8,128)(2,1)S(1)}, u32[]{:S(2)}, u32[]{:S(2)}) collective-permute-start(bf16[2,64,1792]{2,1,0:T(8,128)(2,1)S(1)} %pad_maximum_fusion.2.refs_0_), channel_id=1, source_target_pairs={{0,64},{32,96},{64,0},{96,32},{1,65},{33,97},{65,1},{97,33},{2,66}... | collective-permute-start | bytes 1376264 | tf_op jit(solution)/shard_map/ppermute | solution.py:19
  422.6 36.5 %collective-permute-start.88 = (bf16[2,64,1792]{2,1,0:T(8,128)(2,1)S(1)}, bf16[2,64,1792]{2,1,0:T(8,128)(2,1)S(1)}, u32[]{:S(2)}, u32[]{:S(2)}) collective-permute-start(bf16[2,64,1792]{2,1,0:T(8,128)(2,1)S(1)} %pad_maximum_fusion.2.refs_0_), channel_id=1, source_target_pairs={{0,96},{32,0},{64,32},{96,64},{1,97},{33,1},{65,33},{97,65},{2,98}... | collective-permute-start | bytes 1376264 | tf_op jit(solution)/shard_map/ppermute | solution.py:19
  422.8 17.3 %collective-permute-start.73 = (bf16[64,896]{1,0:T(8,128)(2,1)S(1)}, bf16[64,896]{1,0:T(8,128)(2,1)S(1)}, u32[]{:S(2)}, u32[]{:S(2)}) collective-permute-start(bf16[64,896]{1,0:T(8,128)(2,1)S(1)} %get-tuple-element.127.refs_0_), channel_id=1, source_target_pairs={{0,32},{32,64},{64,96},{96,0},{1,33},{33,65},{65,97},{97,1},{2,34}... | collective-permute-start | bytes 344072 | tf_op jit(solution)/shard_map/ppermute | solution.py:19
  424.6 16.7 %collective-permute-start.74 = (bf16[64,896]{1,0:T(8,128)(2,1)S(1)}, bf16[64,896]{1,0:T(8,128)(2,1)S(1)}, u32[]{:S(2)}, u32[]{:S(2)}) collective-permute-start(bf16[64,896]{1,0:T(8,128)(2,1)S(1)} %get-tuple-element.127.refs_0_), channel_id=1, source_target_pairs={{0,64},{32,96},{64,0},{96,32},{1,65},{33,97},{65,1},{97,33},{2,66}... | collective-permute-start | bytes 344072 | tf_op jit(solution)/shard_map/ppermute | solution.py:19
  447.7 18.7 %collective-permute-start.82 = (bf16[32,2048]{1,0:T(8,128)(2,1)S(1)}, bf16[32,2048]{1,0:T(8,128)(2,1)S(1)}, u32[]{:S(2)}, u32[]{:S(2)}) collective-permute-start(bf16[32,2048]{1,0:T(8,128)(2,1)S(1)} %get-tuple-element.135), channel_id=1, source_target_pairs={{0,7},{1,0},{2,1},{3,2},{4,3},{5,4},{6,5},{7,6},{8,15},{9,8},{10,9... | collective-permute-start | bytes 393224 | tf_op jit(solution)/shard_map/ppermute | solution.py:19
  452.3 14.2 %collective-permute-start.81 = (bf16[32,2048]{1,0:T(8,128)(2,1)S(1)}, bf16[32,2048]{1,0:T(8,128)(2,1)S(1)}, u32[]{:S(2)}, u32[]{:S(2)}) collective-permute-start(bf16[32,2048]{1,0:T(8,128)(2,1)S(1)} %get-tuple-element.134), channel_id=1, source_target_pairs={{0,6},{1,7},{2,0},{3,1},{4,2},{5,3},{6,4},{7,5},{8,14},{9,15},{10,... | collective-permute-start | bytes 393224 | tf_op jit(solution)/shard_map/ppermute | solution.py:19
  459.1 12.1 %collective-permute-start.79 = (bf16[32,2048]{1,0:T(8,128)(2,1)S(1)}, bf16[32,2048]{1,0:T(8,128)(2,1)S(1)}, u32[]{:S(2)}, u32[]{:S(2)}) collective-permute-start(bf16[32,2048]{1,0:T(8,128)(2,1)S(1)} %get-tuple-element.132), channel_id=1, source_target_pairs={{0,4},{1,5},{2,6},{3,7},{4,0},{5,1},{6,2},{7,3},{8,12},{9,13},{10,... | collective-permute-start | bytes 393224 | tf_op jit(solution)/shard_map/ppermute | solution.py:19
  459.2 13.8 %collective-permute-start.78 = (bf16[32,2048]{1,0:T(8,128)(2,1)S(1)}, bf16[32,2048]{1,0:T(8,128)(2,1)S(1)}, u32[]{:S(2)}, u32[]{:S(2)}) collective-permute-start(bf16[32,2048]{1,0:T(8,128)(2,1)S(1)} %get-tuple-element.131), channel_id=1, source_target_pairs={{0,3},{1,4},{2,5},{3,6},{4,7},{5,0},{6,1},{7,2},{8,11},{9,12},{10,... | collective-permute-start | bytes 393224 | tf_op jit(solution)/shard_map/ppermute | solution.py:19
  466.5 11.8 %collective-permute-start.76 = (bf16[32,2048]{1,0:T(8,128)(2,1)S(1)}, bf16[32,2048]{1,0:T(8,128)(2,1)S(1)}, u32[]{:S(2)}, u32[]{:S(2)}) collective-permute-start(bf16[32,2048]{1,0:T(8,128)(2,1)S(1)} %get-tuple-element.129), channel_id=1, source_target_pairs={{0,1},{1,2},{2,3},{3,4},{4,5},{5,6},{6,7},{7,0},{8,9},{9,10},{10,1... | collective-permute-start | bytes 393224 | tf_op jit(solution)/shard_map/ppermute | solution.py:19
  473.0 12.2 %collective-permute-start.93 = (bf16[256,256]{1,0:T(8,128)(2,1)S(1)}, bf16[256,256]{1,0:T(8,128)(2,1)S(1)}, u32[]{:S(2)}, u32[]{:S(2)}) collective-permute-start(bf16[256,256]{1,0:T(8,128)(2,1)S(1)} %get-tuple-element.145), channel_id=1, source_target_pairs={{0,5},{1,6},{2,7},{3,0},{4,1},{5,2},{6,3},{7,4},{8,13},{9,14},{10,... | collective-permute-start | bytes 393224 | tf_op jit(solution)/shard_map/ppermute | solution.py:19
  (104 other events, 2054.8 us)
